TPU v7x, 32 devices: a whole 2x2x4 slice. The times are simulated.
32 devices in a mesh: shot: 4 (over z), bin: 8 (over y, x, core).
Axes of the slice: x: 2, y: 2, z: 4, core: 2. Of those that a mesh axis runs over, the one named last changes fastest.
Arguments:
- traces: bfloat16 [8192, 2048], P(('shot', 'bin')), may hold values from -6 to 6
- shot_filter: bfloat16 [32, 128], P(('shot', 'bin')), may hold values from -0.5 to 0.5
- channel_gain: float32 [256], replicated, may hold values from 0.5 to 2
- bin_owner: int32 [8192, 1], P(('shot', 'bin')), may hold values from 0 to 31; in each aligned block of 256 rows (0 to 255, 256 to 511, ...) at most 16 rows name the same one
- bin_slot: int32 [8192], P(('shot', 'bin')), may hold values from 0 to 15
- offset_class: int32 [8192], P(('shot', 'bin')), may hold values from 0 to 31
- dip_filter: bfloat16 [9, 31], replicated, may hold values from -0.375 to 0.375
- nmo_start: int32 [32, 2048], replicated, may hold values from 0 to 2040, as said below
- nmo_weights: bfloat16 [32, 8, 2048], replicated, may hold values from -2.09375 to 2.09375
Outputs:
- stacked: float32 [8, 64, 2048], P('shot', 'bin')
Inputs may be any that keep to these rules, and one draw needn't show every extreme that they name: `bin_owner`: among the rows of one device, at most 16 name any one block. `nmo_start`: band starts leave room for all 8 taps and lie at most 64 samples before their output sample.
All inputs are finite; a program needn't handle non-finite values.
Results may differ from a plain program's by a relative error of at most 0.0042.
Values may be sent and summed in bfloat16 or wider, within the bound.
A program may use at most 256 MiB of HBM per device.

v0:
```python
import math

import jax
import jax.numpy as jnp
from jax import lax
from jax.sharding import PartitionSpec as P

IL_DEV = 2
XL_DEV = 8


def padded_2(cells, sides, width):
    for axis, dim in sides:
        count = lax.axis_size(axis)
        ends = count - 1
        head = lax.slice_in_dim(cells, 0, width, axis=dim)
        tail = lax.slice_in_dim(cells, cells.shape[dim] - width, cells.shape[dim], axis=dim)
        cells = jnp.concatenate(
            [
                lax.ppermute(tail, axis, [(i, (i + 1) % count) for i in range(ends)]),
                cells,
                lax.ppermute(head, axis, [((i + 1) % count, i) for i in range(ends)]),
            ],
            axis=dim,
        )
    return cells


def later_block(values):
    pad_zero = jnp.zeros_like(values[..., :1, :])
    return jnp.concatenate((pad_zero, values[..., :-1, :]), axis=-2)


def earlier_block(values):
    pad_zero = jnp.zeros_like(values[..., :1, :])
    return jnp.concatenate((values[..., 1:, :], pad_zero), axis=-2)


def decon_matrices_of(shot_filter):
    row_index = jnp.arange(128, dtype=jnp.int32)[:, None]
    col_index = jnp.arange(256, dtype=jnp.int32)[None, :]
    lag_index = col_index % 128 - row_index - 128 * (col_index // 128 - 1)
    valid = (lag_index >= 0) & (lag_index < 128)
    picked = jnp.take(shot_filter, jnp.clip(lag_index, 0, 127).reshape(-1), axis=1).reshape(
        shot_filter.shape[0], 128, 256
    )
    return jnp.where(valid[None], picked, jnp.zeros((), shot_filter.dtype))


def dip_matrices_of(dip_filter):
    time_taps = dip_filter.shape[1]
    row_index = jnp.arange(128, dtype=jnp.int32)[:, None]
    col_index = jnp.arange(384, dtype=jnp.int32)[None, :]
    difference = 128 * (col_index // 128 - 1) + row_index - col_index % 128 + time_taps // 2
    valid = (difference >= 0) & (difference < time_taps)
    picked = jnp.take(
        dip_filter, jnp.clip(difference, 0, time_taps - 1).reshape(-1), axis=1
    ).reshape(dip_filter.shape[0], 128, 384)
    return jnp.where(valid[None], picked, jnp.zeros((), dip_filter.dtype))


def dip_sum(padded, matrices, out_width):
    lead = padded.shape[0]
    offsets = padded.shape[2]
    blocks = padded.shape[3] // 128
    block_shape = (lead, out_width, offsets, blocks, 128)
    summed = jnp.zeros(block_shape, jnp.float32)
    for tap_index in range(matrices.shape[0]):
        trace_rows = padded[:, tap_index : tap_index + out_width].reshape(-1, 128)
        before = jnp.dot(
            trace_rows, matrices[tap_index, :, :128], preferred_element_type=jnp.float32
        ).reshape(block_shape)
        centre = jnp.dot(
            trace_rows, matrices[tap_index, :, 128:256], preferred_element_type=jnp.float32
        ).reshape(block_shape)
        following = jnp.dot(
            trace_rows, matrices[tap_index, :, 256:], preferred_element_type=jnp.float32
        ).reshape(block_shape)
        summed = summed + later_block(before) + centre + earlier_block(following)
    return summed


def band_matrices(band_start, weights):
    offsets, samples = band_start.shape
    blocks = samples // 128
    block_index = jnp.arange(blocks, dtype=jnp.int32)[:, None, None]
    window_row = jnp.arange(384, dtype=jnp.int32)[None, :, None]
    out_col = jnp.arange(128, dtype=jnp.int32)[None, None, :]
    input_sample = 128 * (block_index - 1) + window_row
    starts = band_start.reshape(offsets, blocks, 1, 128)
    banded = jnp.zeros((offsets, blocks, 384, 128), jnp.bfloat16)
    for tap_index in range(weights.shape[1]):
        tap_weight = weights[:, tap_index, :].reshape(offsets, blocks, 1, 128)
        hit = starts + tap_index == input_sample[None] + 0 * out_col[None]
        banded = banded + jnp.where(hit, tap_weight, jnp.zeros((), jnp.bfloat16))
    return banded


def move_out(filtered, band_start, weights):
    rows, offsets, samples = filtered.shape
    blocks = samples // 128
    group = 8
    groups = offsets // group
    grouped = filtered.reshape(rows, groups, group, samples).transpose(1, 0, 2, 3)
    grouped_start = band_start.reshape(groups, group, samples)
    grouped_weights = weights.reshape(groups, group, weights.shape[1], samples)

    def add_group(total, pieces):
        block_data, start_part, weight_part = pieces
        banded = band_matrices(start_part, weight_part)
        padded = jnp.pad(block_data, ((0, 0), (0, 0), (128, 128))).reshape(
            rows, group, blocks + 2, 128
        )
        window = jnp.concatenate((padded[:, :, :-2], padded[:, :, 1:-1], padded[:, :, 2:]), axis=-1)
        term = jnp.einsum("bojr,ojrn->bjn", window, banded, preferred_element_type=jnp.float32)
        return (total + term, None)

    start_total = jnp.zeros((rows, blocks, 128), jnp.float32)
    total, unused = lax.scan(add_group, start_total, (grouped, grouped_start, grouped_weights))
    return total.reshape(rows, samples) / math.sqrt(offsets)


def per_device(
    traces,
    shot_filter,
    channel_gain,
    bin_owner,
    bin_slot,
    offset_class,
    dip_filter,
    nmo_start,
    nmo_weights,
):
    owners = lax.axis_size("shot") * lax.axis_size("bin")
    trace_count = traces.shape[0]
    capacity = 2 * trace_count // owners
    samples = traces.shape[1]
    blocks = samples // 128
    shots_here = shot_filter.shape[0]
    channels = channel_gain.shape[0]
    offsets = nmo_start.shape[0]
    decon_matrices = decon_matrices_of(shot_filter)
    shot_rows = traces.reshape(shots_here, channels * blocks, 128)
    product = jnp.einsum(
        "srq,sqn->srn", shot_rows, decon_matrices, preferred_element_type=jnp.float32
    ).reshape(shots_here, channels, blocks, 256)
    convolved = later_block(product[..., :128]) + product[..., 128:]
    deconvolved = (
        (convolved * channel_gain[None, :, None, None])
        .astype(jnp.bfloat16)
        .reshape(trace_count, samples)
    )
    owner_index = bin_owner[:, 0]
    matches = (owner_index[:, None] == jnp.arange(owners, dtype=jnp.int32)[None, :]).astype(
        jnp.int32
    )
    ranking = jnp.sum(matches * (jnp.cumsum(matches, axis=0) - 1), axis=1)
    position = owner_index * capacity + ranking
    slot_count = owners * capacity
    source = (
        jnp.full((slot_count,), -1, jnp.int32)
        .at[position]
        .set(jnp.arange(trace_count, dtype=jnp.int32))
    )
    filled = source >= 0
    safe_source = jnp.maximum(source, 0)
    outgoing = jnp.where(filled[:, None], deconvolved[safe_source], 0)
    cell_code = bin_slot * offsets + offset_class
    outgoing_cells = jnp.where(filled, cell_code[safe_source], -1)
    arrived, arrived_cells = (
        lax.all_to_all(outgoing, ("shot", "bin"), split_axis=0, concat_axis=0, tiled=True),
        lax.all_to_all(outgoing_cells, ("shot", "bin"), split_axis=0, concat_axis=0, tiled=True),
    )
    cells_here = IL_DEV * XL_DEV * offsets
    member = arrived_cells[None, :] == jnp.arange(cells_here, dtype=jnp.int32)[:, None]
    summed = jnp.dot(member.astype(jnp.bfloat16), arrived, preferred_element_type=jnp.float32)
    fold_count = jnp.sum(member.astype(jnp.float32), axis=1)
    binned = (
        (summed / jnp.maximum(fold_count, 1.0)[:, None])
        .astype(jnp.bfloat16)
        .reshape(IL_DEV, XL_DEV, offsets, samples)
    )
    dip_matrices = dip_matrices_of(dip_filter)
    rim_width = dip_filter.shape[0] // 2
    extended = padded_2(binned, (("bin", 1),), rim_width)
    summed_dip = dip_sum(extended, dip_matrices, XL_DEV)
    filtered = summed_dip.reshape(IL_DEV * XL_DEV, offsets, samples).astype(jnp.bfloat16)
    stacked = move_out(filtered, nmo_start, nmo_weights)
    return stacked.reshape(IL_DEV, XL_DEV, samples)


def solution(mesh):
    placed = (
        P(("shot", "bin"), None),
        P(("shot", "bin"), None),
        P(),
        P(("shot", "bin"), None),
        P(("shot", "bin")),
        P(("shot", "bin")),
        P(),
        P(),
        P(),
    )
    return jax.shard_map(
        per_device, mesh=mesh, in_specs=placed, out_specs=P("shot", "bin", None), check_vma=False
    )
```

profile of v0, /device:TPU:11, one launch (start us, length us, event | category | flops | bytes accessed | tf_op | source)
XLA Modules:
  0.0 661.7 jit_solution(2014639884694361434)
XLA Ops:
  5.1 3.5 gather_fusion
  9.3 6.3 all-to-all-start
  16.2 191.6 %gather_fusion.1 = bf16[32768]{0:T(1024)(128)(2,1)S(1)} fusion(bf16[128]{0:T(256)(128)(2,1)S(1)} %bitcast.352, s32[32768]{0:T(1024)S(1)} %broadcast_clamp_fusion.1), kind=kCustom, calls=%fused_computation.1 | custom fusion | bytes 262144 | tf_op jit(solution)/shard_map/jit(_take)/gather | solution.py:44
  211.8 5.6 copy.82
  225.3 5.9 all-to-all-start.1
  231.5 172.1 %gather_fusion.3 = bf16[49152,9]{1,0:T(8,128)(2,1)} fusion(bf16[9,31]{0,1:T(8,128)(2,1)S(1)} %copy.83, s32[49152]{0:T(1024)S(1)} %broadcast_clamp_fusion), kind=kCustom, calls=%fused_computation.3 | custom fusion | bytes 1966080 | tf_op jit(solution)/shard_map/jit(_take)/gather | solution.py:56
  403.7 10.6 %copy.116 = bf16[9,128,384]{2,1,0:T(8,128)(2,1)S(1)} copy(bf16[9,128,384]{0,2,1:T(8,128)(2,1)} %bitcast.387) | data formatting | bytes 1769472 | tf_op jit(solution)/shard_map/jit(_take)/gather | solution.py:56
  416.0 2.8 divide_convert_fusion
  419.0 3.3 collective-permute-start
  425.6 2.7 fusion.59
  431.0 11.5 %collective-permute-done = bf16[2,4,32,2048]{3,2,1,0:T(8,128)(2,1)S(1)} collective-permute-done((bf16[2,4,32,2048]{3,2,1,0:T(8,128)(2,1)S(1)}, bf16[2,4,32,2048]{3,2,1,0:T(8,128)(2,1)S(1)}, u32[]{:S(2)}, u32[]{:S(2)}) %collective-permute-start) | collective-permute-done | bytes 1048608 | tf_op jit(solution)/shard_map/ppermute | solution.py:20
  442.5 4.5 collective-permute-done.1
  449.5 2.7 fusion.45
  455.4 2.7 fusion.49
  461.3 2.8 fusion.53
  487.0 2.7 fusion.69
  495.6 2.9 fusion.73
  515.1 34.2 %add_convert_fusion = bf16[2,8,32,16,128]{4,3,2,1,0:T(8,128)(2,1)} fusion(f32[2,8,32,15,128]{4,3,2,1,0:T(8,128)} %fusion.41, f32[2,8,32,15,128]{4,3,2,1,0:T(8,128)} %fusion.43, f32[2,8,32,15,128]{4,3,2,1,0:T(8,128)} %fusion.45, f32[2,8,32,16,128]{4,3,2,1,0:T(8,128)} %fusion.96, f32[2,8,32,15,128]{4,3,2,1,0:T(8,128)} %fusion.47, ...), kind=kOutput, calls=%fused_computation.68 | convolution fusion | flops 296747008 | bytes 108822528 | tf_op jit(solution)/shard_map/dot_general | solution.py:73
  549.2 2.8 convert_element_type.33
  553.6 107.4 %while.13 = (s32[]{:T(128)}, f32[16,16,128]{2,0,1:T(8,128)S(1)}, s32[4,8,2048]{2,1,0:T(8,128)}, bf16[4,8,8,2048]{3,2,1,0:T(8,128)(2,1)}, bf16[4,16,8,2048]{3,2,1,0:T(8,128)(2,1)}, /*index=5*/s32[]{:T(128)}, s32[]{:T(128)}) while((s32[]{:T(128)}, f32[16,16,128]{2,0,1:T(8,128)S(1)}, s32[4,8,2048]{2,1,0:T(8,128)}, ...), condition=%wide.region_6.7_spmd.clone, body=%wide.region_5.6_spmd.clone.sunk | while | flops 407558176 | bytes 13353187 | solution.py:119
  558.1 22.3 %fusion.141 = f32[16,16,128]{2,0,1:T(8,128)S(1)} fusion(s32[8,16,128]{2,0,1:T(8,128)S(1)} %get-tuple-element.207, s32[8,16,128]{2,0,1:T(8,128)S(1)} %get-tuple-element.208, s32[8,16,128]{2,0,1:T(8,128)S(1)} %get-tuple-element.209, s32[8,16,128]{2,0,1:T(8,128)S(1)} %get-tuple-element.210, s32[8,16,128]{2,0,1:T(8,128)S(1)} %get-tuple-element.211, ...), kind=kOutput, calls=%fused_computation.36.clone.1 | convolution fusion | flops 407437312 | bytes 2646017 | tf_op jit(solution)/shard_map/while/body/eval_jaxpr/bojr,ojrn->bjn/dot_general | solution.py:115
  585.0 22.3 %fusion.141 = f32[16,16,128]{2,0,1:T(8,128)S(1)} fusion(s32[8,16,128]{2,0,1:T(8,128)S(1)} %get-tuple-element.207, s32[8,16,128]{2,0,1:T(8,128)S(1)} %get-tuple-element.208, s32[8,16,128]{2,0,1:T(8,128)S(1)} %get-tuple-element.209, s32[8,16,128]{2,0,1:T(8,128)S(1)} %get-tuple-element.210, s32[8,16,128]{2,0,1:T(8,128)S(1)} %get-tuple-element.211, ...), kind=kOutput, calls=%fused_computation.36.clone.1 | convolution fusion | flops 407437312 | bytes 2646017 | tf_op jit(solution)/shard_map/while/body/eval_jaxpr/bojr,ojrn->bjn/dot_general | solution.py:115
  611.8 22.3 %fusion.141 = f32[16,16,128]{2,0,1:T(8,128)S(1)} fusion(s32[8,16,128]{2,0,1:T(8,128)S(1)} %get-tuple-element.207, s32[8,16,128]{2,0,1:T(8,128)S(1)} %get-tuple-element.208, s32[8,16,128]{2,0,1:T(8,128)S(1)} %get-tuple-element.209, s32[8,16,128]{2,0,1:T(8,128)S(1)} %get-tuple-element.210, s32[8,16,128]{2,0,1:T(8,128)S(1)} %get-tuple-element.211, ...), kind=kOutput, calls=%fused_computation.36.clone.1 | convolution fusion | flops 407437312 | bytes 2646017 | tf_op jit(solution)/shard_map/while/body/eval_jaxpr/bojr,ojrn->bjn/dot_general | solution.py:115
  638.7 22.3 %fusion.141 = f32[16,16,128]{2,0,1:T(8,128)S(1)} fusion(s32[8,16,128]{2,0,1:T(8,128)S(1)} %get-tuple-element.207, s32[8,16,128]{2,0,1:T(8,128)S(1)} %get-tuple-element.208, s32[8,16,128]{2,0,1:T(8,128)S(1)} %get-tuple-element.209, s32[8,16,128]{2,0,1:T(8,128)S(1)} %get-tuple-element.210, s32[8,16,128]{2,0,1:T(8,128)S(1)} %get-tuple-element.211, ...), kind=kOutput, calls=%fused_computation.36.clone.1 | convolution fusion | flops 407437312 | bytes 2646017 | tf_op jit(solution)/shard_map/while/body/eval_jaxpr/bojr,ojrn->bjn/dot_general | solution.py:115
  (147 shorter events, 100.5 us)
Async XLA Ops:
  0.0 16.2 %copy-start = (bf16[1,128]{1,0:T(2,128)(2,1)S(1)}, bf16[1,128]{1,0:T(2,128)(2,1)}, u32[]{:S(2)}) copy-start(bf16[1,128]{1,0:T(2,128)(2,1)} %param.12) | copy-start | bytes 772
  9.3 215.9 %all-to-all-start = ((s32[32,16,1]{1,2,0:T(1,128)}), s32[32,16,1]{1,2,0:T(1,128)S(1)}, u32[]{:S(2)}, u32[]{:S(2)}) async-start(s32[32,16,1]{1,2,0:T(1,128)} %bitcast.7), calls=%async_computation | async-start | bytes 32768 | tf_op jit(solution)/shard_map/all_to_all | solution.py:172
  16.2 192.3 %copy-start.3 = (bf16[256,2048]{1,0:T(8,128)(2,1)S(1)}, bf16[256,2048]{1,0:T(8,128)(2,1)}, u32[]{:S(2)}) copy-start(bf16[256,2048]{1,0:T(8,128)(2,1)} %param.11) | copy-start | bytes 3145732
  217.4 2.8 copy-start.2
  217.4 2.8 copy-start.5
  225.0 6.4 copy-start.4
  225.3 190.8 %all-to-all-start.1 = ((bf16[32,16,2048]{2,1,0:T(8,128)(2,1)}), bf16[32,16,2048]{2,1,0:T(8,128)(2,1)}, u32[]{:S(2)}, u32[]{:S(2)}) async-start(bf16[32,16,2048]{2,1,0:T(8,128)(2,1)} %broadcast_select_fusion), calls=%async_computation.1 | async-start | bytes 4194304 | tf_op jit(solution)/shard_map/all_to_all | solution.py:171
  419.0 23.5 %collective-permute-start = (bf16[2,4,32,2048]{3,2,1,0:T(8,128)(2,1)S(1)}, bf16[2,4,32,2048]{3,2,1,0:T(8,128)(2,1)S(1)}, u32[]{:S(2)}, u32[]{:S(2)}) collective-permute-start(bf16[2,4,32,2048]{3,2,1,0:T(8,128)(2,1)S(1)} %get-tuple-element.148), channel_id=1, source_target_pairs={{0,1},{1,2},{2,3},{3,4},{4,5},{5,6},{6,7},{8,9},{9,10},{10,11},{11... | collective-permute-start | bytes 3145736 | tf_op jit(solution)/shard_map/ppermute | solution.py:20
  422.4 24.6 %collective-permute-start.1 = (bf16[2,4,32,2048]{3,2,1,0:T(8,128)(2,1)S(1)}, bf16[2,4,32,2048]{3,2,1,0:T(8,128)(2,1)S(1)}, u32[]{:S(2)}, u32[]{:S(2)}) collective-permute-start(bf16[2,4,32,2048]{3,2,1,0:T(8,128)(2,1)S(1)} %get-tuple-element.149), channel_id=1, source_target_pairs={{1,0},{2,1},{3,2},{4,3},{5,4},{6,5},{7,6},{9,8},{10,9},{11,10},{12... | collective-permute-start | bytes 3145736 | tf_op jit(solution)/shard_map/ppermute | solution.py:22
  661.0 0.8 copy-start.1
where the time goes:
time: 664 us; the launch traced here: 662 us
  local copies, waits for them, and re-layouts  418 us (63%)
  matrix products  196 us (30%)
  starting transfers between devices  17.5 us (3%)
  waiting for transfers between devices  16 us (2%)
  other arithmetic  13.5 us (2%)
    gather x1, local copies, waits for them, and re-layouts, decon_matrices_of(): jnp.take(shot_filter, jnp.clip(lag_index, 0, 127).reshape(-1), axis=1)  192 us
    gather x2, local copies, waits for them, and re-layouts, dip_matrices_of(): jnp.take(dip_filter, jnp.clip(difference, 0, time_taps - 1).reshape(-1),...  183 us
    dot_general x4, matrix products, add_group(): jnp.einsum('bojr,ojrn->bjn', window, banded, preferred_element_type=jnp.f...  89.2 us
    dot_general x9, matrix products, dip_sum(): jnp.dot(trace_rows, matrices[tap_index, :, 128:256], preferred_element_ty...  55.3 us
    dot_general x9, matrix products, dip_sum(): jnp.dot(trace_rows, matrices[tap_index, :, :128], preferred_element_type=...  23.7 us
    dot_general x9, matrix products, dip_sum(): jnp.dot(trace_rows, matrices[tap_index, :, 256:], preferred_element_type=...  22.4 us
  transfers between devices with their start and end apart: 4, of which 2 were waited for; matrix products, arithmetic and copies ran while one was open for 60% of the time, Pallas kernels for 0%

commit v1 on v0

v1 whole, which is shorter than its diff:
```python
import functools
import math

import jax
import jax.numpy as jnp
from jax import lax
from jax.experimental import pallas as pl
from jax.experimental.pallas import tpu as pltpu
from jax.sharding import PartitionSpec as P

IL_DEV = 2
XL_DEV = 8
MESH = pl.DeviceIdType.MESH
AXES = ("shot", "bin")
VMEM_BYTES = 40 * 1024 * 1024


def iota(shape, dim):
    return lax.broadcasted_iota(jnp.int32, shape, dim)


def toeplitz(row):
    return pltpu.roll(jnp.broadcast_to(row, (256, 256)), 0, 1, stride=1, stride_axis=0)


def decon_kernel(owners, capacity, traces, filters, gain, owner_row, out, dec):
    trace_count, samples = traces.shape
    shots = filters.shape[0]
    channels = gain.shape[0]
    for shot in range(shots):
        taps = filters[shot : shot + 1, :].astype(jnp.float32)
        matrix = toeplitz(jnp.concatenate([jnp.zeros_like(taps), taps], axis=1))[:, :128]
        matrix = matrix.astype(jnp.bfloat16)
        rows = slice(shot * channels, (shot + 1) * channels)
        for block in range(samples // 128):
            lanes = slice(128 * block, 128 * block + 128)
            if block == 0:
                product = jnp.dot(
                    traces[rows, lanes], matrix[128:], preferred_element_type=jnp.float32
                )
            else:
                window = slice(128 * block - 128, 128 * block + 128)
                product = jnp.dot(
                    traces[rows, window], matrix, preferred_element_type=jnp.float32
                )
            dec[rows, lanes] = (product * gain[...]).astype(jnp.bfloat16)
    hit = iota((owners, trace_count), 0) == owner_row[...]
    hit_f = jnp.where(hit, 1.0, 0.0)
    upper = iota((trace_count, trace_count), 0) <= iota((trace_count, trace_count), 1)
    running = jnp.dot(
        hit_f.astype(jnp.bfloat16),
        jnp.where(upper, 1.0, 0.0).astype(jnp.bfloat16),
        preferred_element_type=jnp.float32,
    )
    rank = jnp.sum(jnp.where(hit, running - 1.0, 0.0), axis=0, keepdims=True)
    position = owner_row[...] * capacity + rank.astype(jnp.int32)
    slots = owners * capacity
    pick = jnp.where(iota((slots, trace_count), 0) == position, 1.0, 0.0).astype(jnp.bfloat16)
    for lane in range(0, samples, 256):
        out[:, lane : lane + 256] = jnp.dot(
            pick, dec[:, lane : lane + 256], preferred_element_type=jnp.float32
        ).astype(jnp.bfloat16)


def exchange_kernel(shots, bins, out_ref, in_ref, send_sem, recv_sem, own_sem):
    count = shots * bins
    me = lax.axis_index("shot") * bins + lax.axis_index("bin")
    barrier = pltpu.get_barrier_semaphore()

    def greet(step, carry):
        other = lax.rem(me + step, count)
        pl.semaphore_signal(
            barrier, inc=1, device_id=(other // bins, lax.rem(other, bins)), device_id_type=MESH
        )
        return carry

    lax.fori_loop(1, count, greet, 0)
    own = pltpu.make_async_copy(out_ref.at[me], in_ref.at[me], own_sem)
    own.start()
    pl.semaphore_wait(barrier, count - 1)

    def copy_of(step):
        other = lax.rem(me + step, count)
        return pltpu.make_async_remote_copy(
            src_ref=out_ref.at[other],
            dst_ref=in_ref.at[me],
            send_sem=send_sem.at[step],
            recv_sem=recv_sem.at[step],
            device_id=(other // bins, lax.rem(other, bins)),
            device_id_type=MESH,
        )

    def begin(step, carry):
        copy_of(step).start()
        return carry

    def finish(step, carry):
        copy_of(step).wait()
        return carry

    lax.fori_loop(1, count, begin, 0)
    own.wait()
    lax.fori_loop(1, count, finish, 0)


def exchange(outgoing, collective_id):
    shots, bins = lax.axis_size("shot"), lax.axis_size("bin")
    count = shots * bins
    return pl.pallas_call(
        functools.partial(exchange_kernel, shots, bins),
        out_shape=jax.ShapeDtypeStruct(outgoing.shape, outgoing.dtype),
        in_specs=[pl.BlockSpec(memory_space=pl.ANY)],
        out_specs=pl.BlockSpec(memory_space=pl.ANY),
        scratch_shapes=[
            pltpu.SemaphoreType.DMA((count,)),
            pltpu.SemaphoreType.DMA((count,)),
            pltpu.SemaphoreType.DMA,
        ],
        compiler_params=pltpu.CompilerParams(
            collective_id=collective_id, has_side_effects=True
        ),
        name="exchange",
    )(outgoing)


def bin_kernel(capacity, cells_here, arrived, codes, lo, hi):
    owners, trace_count = codes.shape
    slots, samples = arrived.shape
    local = codes[...]
    mine = (local >= 0) & (local < cells_here)
    upper = iota((trace_count, trace_count), 0) <= iota((trace_count, trace_count), 1)
    running = jnp.dot(
        jnp.where(mine, 1.0, 0.0).astype(jnp.bfloat16),
        jnp.where(upper, 1.0, 0.0).astype(jnp.bfloat16),
        preferred_element_type=jnp.float32,
    )
    ranked = jnp.where(mine, running, 0.0)
    named = local.astype(jnp.float32) + 1.0
    place = iota((owners, slots), 1) - capacity * iota((owners, slots), 0)
    spread = jnp.zeros((owners, slots), jnp.float32)
    for rank in range(capacity):
        code = jnp.sum(jnp.where(ranked == rank + 1.0, named, 0.0), axis=1, keepdims=True)
        spread = jnp.where(place == rank, code, spread)
    slot_code = jnp.sum(spread, axis=0, keepdims=True).astype(jnp.int32)
    member_f = jnp.where(iota((cells_here, slots), 0) + 1 == slot_code, 1.0, 0.0)
    fold = jnp.sum(member_f, axis=1, keepdims=True)
    scale = 1.0 / jnp.maximum(fold, 1.0)
    member = member_f.astype(jnp.bfloat16)
    offsets = lo.shape[2]
    half = XL_DEV // 2
    for lane in range(0, samples, 256):
        summed = jnp.dot(
            member, arrived[:, lane : lane + 256], preferred_element_type=jnp.float32
        )
        binned = (summed * scale).astype(jnp.bfloat16).reshape(IL_DEV, XL_DEV, offsets, 256)
        lo[:, :, :, lane : lane + 256] = binned[:, :half]
        hi[:, :, :, lane : lane + 256] = binned[:, half:]


def stack_kernel(
    taps, left, lo, hi, right, dip_rows, start, weights, out, ext, matrix, filtered, sems
):
    crosslines = ext.shape[1]
    offsets = ext.shape[2]
    samples = ext.shape[3] - 256
    blocks = samples // 128
    half = crosslines // 4
    copies = []
    for part, ref in enumerate((left, lo, hi, right)):
        copy = pltpu.make_async_copy(
            ref,
            ext.at[:, part * half : part * half + half, :, 128 : 128 + samples],
            sems.at[part],
        )
        copy.start()
        copies.append(copy)
    zero = jnp.zeros((IL_DEV, crosslines, offsets, 128), jnp.bfloat16)
    ext[:, :, :, :128] = zero
    ext[:, :, :, 128 + samples :] = zero
    matrix[...] = jnp.zeros(matrix.shape, jnp.bfloat16)
    for tap in range(taps):
        one = toeplitz(dip_rows[tap : tap + 1, :])[:, :128].astype(jnp.bfloat16)
        matrix[256 * tap : 256 * tap + 256, :128] = one
        matrix[256 * tap + 256 : 256 * tap + 512, 128:] = one
    for copy in copies:
        copy.wait()
    pairs = XL_DEV // 2

    def filter_block(block, carry):
        lanes = pl.ds(pl.multiple_of(128 * block, 128), 256)
        window = ext[:, :, :, lanes].reshape(IL_DEV, crosslines // 2, 2, offsets, 256)
        pieces = []
        for tap in range(taps + 1):
            piece = window[:, tap // 2 : tap // 2 + pairs, tap % 2]
            pieces.append(piece.reshape(IL_DEV * pairs * offsets, 256))
        result = jnp.dot(
            jnp.concatenate(pieces, axis=1), matrix[...], preferred_element_type=jnp.float32
        )
        rounded = result.astype(jnp.bfloat16).astype(jnp.float32)
        for side in range(2):
            filtered[block, :, :, side] = rounded[:, 128 * side : 128 * side + 128].reshape(
                IL_DEV, pairs, offsets, 128
            )
        return carry

    lax.fori_loop(0, blocks + 1, filter_block, 0)
    nmo_taps = weights.shape[0]
    scale = 1.0 / math.sqrt(offsets)

    def stack_block(block, carry):
        lanes = pl.ds(pl.multiple_of(128 * block, 128), 128)
        totals = [jnp.zeros((8, 128), jnp.float32) for _ in range(IL_DEV * XL_DEV)]
        for first in range(0, offsets, 8):
            group = slice(first, first + 8)
            at = start[group, lanes] - (128 * block - 64)
            index, early, weight = [], [], []
            for tap in range(nmo_taps):
                moved = at + tap
                index.append(moved & 127)
                early.append(moved < 128)
                weight.append(weights[tap, group, lanes])
            for cell in range(IL_DEV * XL_DEV):
                place = (cell // XL_DEV, cell % XL_DEV // 2, cell % 2)
                here = filtered[(block,) + place + (group, slice(None))]
                after = filtered[(block + 1,) + place + (group, slice(None))]
                for tap in range(nmo_taps):
                    value = jnp.where(
                        early[tap],
                        jnp.take_along_axis(here, index[tap], axis=1),
                        jnp.take_along_axis(after, index[tap], axis=1),
                    )
                    totals[cell] = totals[cell] + value * weight[tap]
        for inline in range(IL_DEV):
            rows = [
                jnp.sum(totals[inline * XL_DEV + x], axis=0, keepdims=True) for x in range(XL_DEV)
            ]
            out[inline, :, lanes] = jnp.concatenate(rows, axis=0) * scale
        return carry

    lax.fori_loop(0, blocks, stack_block, 0)


def per_device(
    traces,
    shot_filter,
    channel_gain,
    bin_owner,
    bin_slot,
    offset_class,
    dip_filter,
    nmo_start,
    nmo_weights,
):
    bins = lax.axis_size("bin")
    owners = lax.axis_size("shot") * bins
    me = lax.axis_index("shot") * bins + lax.axis_index("bin")
    trace_count, samples = traces.shape
    capacity = 2 * trace_count // owners
    slots = owners * capacity
    offsets = nmo_start.shape[0]
    cells_here = IL_DEV * XL_DEV * offsets
    half = XL_DEV // 2
    vmem = pl.BlockSpec(memory_space=pltpu.VMEM)
    anywhere = pl.BlockSpec(memory_space=pl.ANY)
    params = pltpu.CompilerParams(vmem_limit_bytes=VMEM_BYTES)

    owner = bin_owner[:, 0]
    code = owner * cells_here + bin_slot * offsets + offset_class
    codes = lax.all_gather(code, AXES) - me * cells_here

    outgoing = pl.pallas_call(
        functools.partial(decon_kernel, owners, capacity),
        out_shape=jax.ShapeDtypeStruct((slots, samples), jnp.bfloat16),
        in_specs=[vmem] * 4,
        out_specs=vmem,
        scratch_shapes=[pltpu.VMEM((trace_count, samples), jnp.bfloat16)],
        compiler_params=params,
        name="decon",
    )(traces, shot_filter, channel_gain[:, None], owner[None, :])

    arrived = exchange(outgoing.reshape(owners, capacity, samples), 1)

    rim = jax.ShapeDtypeStruct((IL_DEV, half, offsets, samples), jnp.bfloat16)
    lo, hi = pl.pallas_call(
        functools.partial(bin_kernel, capacity, cells_here),
        out_shape=(rim, rim),
        in_specs=[vmem] * 2,
        out_specs=(vmem, vmem),
        compiler_params=params,
        name="bin",
    )(arrived.reshape(slots, samples), codes)

    right = lax.ppermute(lo, "bin", [(i + 1, i) for i in range(bins - 1)])
    left = lax.ppermute(hi, "bin", [(i, i + 1) for i in range(bins - 1)])

    taps, time_taps = dip_filter.shape
    before = 192 + time_taps // 2 - (time_taps - 1)
    dip_rows = jnp.pad(
        dip_filter[:, ::-1].astype(jnp.float32),
        ((0, 0), (before, 256 - before - time_taps)),
    )
    weights = jnp.transpose(nmo_weights, (1, 0, 2)).astype(jnp.float32)
    crosslines = 2 * XL_DEV
    return pl.pallas_call(
        functools.partial(stack_kernel, taps),
        out_shape=jax.ShapeDtypeStruct((IL_DEV, XL_DEV, samples), jnp.float32),
        in_specs=[anywhere] * 4 + [vmem] * 3,
        out_specs=vmem,
        scratch_shapes=[
            pltpu.VMEM((IL_DEV, crosslines, offsets, samples + 256), jnp.bfloat16),
            pltpu.VMEM(((taps + 1) * 256, 256), jnp.bfloat16),
            pltpu.VMEM(
                (samples // 128 + 1, IL_DEV, XL_DEV // 2, 2, offsets, 128), jnp.float32
            ),
            pltpu.SemaphoreType.DMA((4,)),
        ],
        compiler_params=params,
        name="stack",
    )(left, lo, hi, right, dip_rows, nmo_start, weights)


def solution(mesh):
    placed = (
        P(AXES, None),
        P(AXES, None),
        P(),
        P(AXES, None),
        P(AXES),
        P(AXES),
        P(),
        P(),
        P(),
    )
    return jax.shard_map(
        per_device, mesh=mesh, in_specs=placed, out_specs=P("shot", "bin", None), check_vma=False
    )
```

time: 664 us -> 189 us (0.28)
  local copies, waits for them, and re-layouts: 418 us -> 6.38 us
  matrix products: 196 us -> 0 us
  Pallas kernels: 0 us -> 117 us
  blocking collectives: 0 us -> 31.3 us
  starting transfers between devices: 17.5 us -> 7.13 us
  other arithmetic: 13.5 us -> 3.3 us
    gather x5 -> x0, local copies, waits for them, and re-layouts: 380 us -> none  [the longest x1 192 us: decon_matrices_of(): jnp.take(shot_filter, jnp.clip(lag_index, 0, 127).reshape(-1), axis=1)]
    dot_general x33 -> x0, matrix products: 196 us -> none  [the longest x4 89.2 us: add_group(): jnp.einsum('bojr,ojrn->bjn', window, banded, preferred_element_type=jnp.f...]
    pallas_call x0 -> x4, Pallas kernels: none -> 117 us  [the longest x1 61.6 us: exchange(): pl.pallas_call(functools.partial(exchange_kernel, shots, bins), out_shape...]
    all_gather x0 -> x1, blocking collectives: none -> 31.3 us  [per_device(): codes = lax.all_gather(code, AXES) - me * cells_here]
    all_to_all x2 -> x0, starting transfers between devices: 12.2 us -> none  [the longest x1 6.33 us: per_device(): lax.all_to_all(outgoing_cells, ('shot', 'bin'), split_axis=0, concat_axis...]
    ppermute x2, waiting for transfers between devices: 16 us -> 22.6 us  [the longest x1 18 us: per_device(): left = lax.ppermute(hi, 'bin', [(i, i + 1) for i in range(bins - 1)])]
  transfers between devices with their start and end apart: 4 -> 2, of which waited for: 2 -> 2; matrix products, arithmetic and copies ran while one was open for 60% -> 1% of each run, Pallas kernels for 0% -> 0%
where the time goes in v1:
time: 189 us; the launch traced here: 188 us
  Pallas kernels  117 us (62%)
  blocking collectives  31.3 us (17%)
  waiting for transfers between devices  22.6 us (12%)
  starting transfers between devices  7.13 us (4%)
  local copies, waits for them, and re-layouts  6.38 us (3%)
  other arithmetic  3.3 us (2%)
    pallas_call x1, Pallas kernels, exchange(): pl.pallas_call(functools.partial(exchange_kernel, shots, bins), out_shape...  61.6 us
    pallas_call x1, Pallas kernels, per_device(): pl.pallas_call(functools.partial(stack_kernel, taps), out_shape=jax.Shape...  52.7 us
    all_gather x1, blocking collectives, per_device(): codes = lax.all_gather(code, AXES) - me * cells_here  31.3 us
    ppermute x1, waiting for transfers between devices, per_device(): left = lax.ppermute(hi, 'bin', [(i, i + 1) for i in range(bins - 1)])  18 us
    unnamed x14, local copies, waits for them, and re-layouts  5.48 us
    ppermute x1, starting transfers between devices, per_device(): left = lax.ppermute(hi, 'bin', [(i, i + 1) for i in range(bins - 1)])  5.21 us
    ppermute x1, waiting for transfers between devices, per_device(): right = lax.ppermute(lo, 'bin', [(i + 1, i) for i in range(bins - 1)])  4.63 us
  transfers between devices with their start and end apart: 2, of which 2 were waited for; matrix products, arithmetic and copies ran while one was open for 1% of the time, Pallas kernels for 0%

profile of v1, /device:TPU:11, one launch (start us, length us, event | category | flops | bytes accessed | tf_op | source)
XLA Modules:
  0.0 188.3 jit_solution(4380434066584494131)
XLA Ops:
  0.0 0.7 broadcast_multiply_fusion
  0.7 0.7 add_add_fusion
  1.4 31.3 %all-gather.1 = s32[32,1,256]{2,1,0:T(1,128)S(1)} all-gather(s32[1,1,256]{2,1,0:T(1,128)S(1)} %bitcast.13), channel_id=2, replica_groups=mesh['shot'=4,'bin'=8] {'shot','bin'}, dimensions={0}, use_global_device_ids=true | all-gather | bytes 33792 | tf_op jit(solution)/shard_map/all_gather | solution.py:269
  32.7 0.8 copy.13.gain
  33.5 0.0 copy-start.2
  33.5 1.2 copy-done.2
  34.7 0.7 copy-done.4
  35.4 0.7 copy-done.5
  36.1 1.5 decon.1
  37.5 0.0 copy-start
  37.6 1.3 copy-done
  38.9 61.6 %exchange.1 = bf16[32,16,2048]{2,1,0:T(8,128)(2,1)} custom-call(bf16[32,16,2048]{2,1,0:T(8,128)(2,1)} %bitcast.10), custom_call_target="tpu_custom_call" | custom-call | tf_op jit(solution)/shard_map/exchange/pallas_call | solution.py:109
  100.5 0.0 copy-start.6
  100.6 1.6 copy-done.1
  102.1 1.6 bin.1
  103.8 0.0 copy-start.3
  103.8 5.2 %collective-permute-start = (bf16[2,4,32,2048]{3,2,1,0:T(8,128)(2,1)S(1)}, bf16[2,4,32,2048]{3,2,1,0:T(8,128)(2,1)S(1)}, u32[]{:S(2)}, u32[]{:S(2)}) collective-permute-start(bf16[2,4,32,2048]{3,2,1,0:T(8,128)(2,1)S(1)} %get-tuple-element.7.hi), channel_id=1, source_target_pairs={{0,1},{1,2},{2,3},{3,4},{4,5},{5,6},{6,7},{8,9},{9,10},{10,11},{11... | collective-permute-start | bytes 3145736 | tf_op jit(solution)/shard_map/ppermute | solution.py:294
  109.0 1.9 %collective-permute-start.1 = (bf16[2,4,32,2048]{3,2,1,0:T(8,128)(2,1)S(1)}, bf16[2,4,32,2048]{3,2,1,0:T(8,128)(2,1)}, u32[]{:S(2)}, u32[]{:S(2)}) collective-permute-start(bf16[2,4,32,2048]{3,2,1,0:T(8,128)(2,1)S(1)} %get-tuple-element.8.lo), channel_id=1, source_target_pairs={{1,0},{2,1},{3,2},{4,3},{5,4},{6,5},{7,6},{9,8},{10,9},{11,10},{12... | collective-permute-start | bytes 3145736 | tf_op jit(solution)/shard_map/ppermute | solution.py:293
  111.0 0.1 rev.3
  111.0 0.1 pad_convert_fusion.dip_rows
  111.1 1.8 convert_bitcast_fusion.weights
  113.0 18.0 %collective-permute-done.left = bf16[2,4,32,2048]{3,2,1,0:T(8,128)(2,1)S(1)} collective-permute-done((bf16[2,4,32,2048]{3,2,1,0:T(8,128)(2,1)S(1)}, bf16[2,4,32,2048]{3,2,1,0:T(8,128)(2,1)S(1)}, u32[]{:S(2)}, u32[]{:S(2)}) %collective-permute-start) | collective-permute-done | bytes 1048608 | tf_op jit(solution)/shard_map/ppermute | solution.py:294
  131.0 4.6 %collective-permute-done.1.right = bf16[2,4,32,2048]{3,2,1,0:T(8,128)(2,1)} collective-permute-done((bf16[2,4,32,2048]{3,2,1,0:T(8,128)(2,1)S(1)}, bf16[2,4,32,2048]{3,2,1,0:T(8,128)(2,1)}, u32[]{:S(2)}, u32[]{:S(2)}) %collective-permute-start.1) | collective-permute-done | bytes 1048608 | tf_op jit(solution)/shard_map/ppermute | solution.py:293
  135.6 52.7 %stack.1 = f32[2,8,2048]{2,1,0:T(8,128)} custom-call(bf16[2,4,32,2048]{3,2,1,0:T(8,128)(2,1)S(1)} %collective-permute-done.left, bf16[2,4,32,2048]{3,2,1,0:T(8,128)(2,1)S(1)} %get-tuple-element.8.lo, bf16[2,4,32,2048]{3,2,1,0:T(8,128)(2,1)S(1)} %get-tuple-element.7.hi, bf16[2,4,32,2048]{3,2,1,0:T(8,128)(2,1)} %collective-permute-done.1.right, ...), custom_call_target="tpu_custom_call" | custom-call | tf_op jit(solution)/shard_map/stack/pallas_call | solution.py:304
  (6 shorter events, 0.0 us)
Async XLA Ops:
  33.5 1.2 copy-start.2
  34.7 0.7 copy-start.4
  35.4 0.7 copy-start.5
  37.5 1.3 copy-start
  100.5 10.4 %copy-start.6 = (bf16[9,31]{1,0:T(8,128)(2,1)S(1)}, bf16[9,31]{1,0:T(8,128)(2,1)}, u32[]{:S(2)}) copy-start(bf16[9,31]{1,0:T(8,128)(2,1)} %param.15) | copy-start | bytes 1678
  100.5 1.6 copy-start.1
  103.8 31.8 %copy-start.3 = (s32[32,2048]{1,0:T(8,128)S(1)}, s32[32,2048]{1,0:T(8,128)}, u32[]{:S(2)}) copy-start(s32[32,2048]{1,0:T(8,128)} %start.1) | copy-start | bytes 786436
  103.8 27.2 %collective-permute-start = (bf16[2,4,32,2048]{3,2,1,0:T(8,128)(2,1)S(1)}, bf16[2,4,32,2048]{3,2,1,0:T(8,128)(2,1)S(1)}, u32[]{:S(2)}, u32[]{:S(2)}) collective-permute-start(bf16[2,4,32,2048]{3,2,1,0:T(8,128)(2,1)S(1)} %get-tuple-element.7.hi), channel_id=1, source_target_pairs={{0,1},{1,2},{2,3},{3,4},{4,5},{5,6},{6,7},{8,9},{9,10},{10,11},{11... | collective-permute-start | bytes 3145736 | tf_op jit(solution)/shard_map/ppermute | solution.py:294
  109.0 26.6 %collective-permute-start.1 = (bf16[2,4,32,2048]{3,2,1,0:T(8,128)(2,1)S(1)}, bf16[2,4,32,2048]{3,2,1,0:T(8,128)(2,1)}, u32[]{:S(2)}, u32[]{:S(2)}) collective-permute-start(bf16[2,4,32,2048]{3,2,1,0:T(8,128)(2,1)S(1)} %get-tuple-element.8.lo), channel_id=1, source_target_pairs={{1,0},{2,1},{3,2},{4,3},{5,4},{6,5},{7,6},{9,8},{10,9},{11,10},{12... | collective-permute-start | bytes 3145736 | tf_op jit(solution)/shard_map/ppermute | solution.py:293

commit v2 on v1

--- a/solution.py
+++ b/solution.py
@@ -23,7 +23,9 @@
     return pltpu.roll(jnp.broadcast_to(row, (256, 256)), 0, 1, stride=1, stride_axis=0)
 
 
-def decon_kernel(owners, capacity, traces, filters, gain, owner_row, out, dec):
+def decon_kernel(
+    owners, capacity, offsets, traces, filters, gain, owner_row, slot_row, class_row, out, codes, dec
+):
     trace_count, samples = traces.shape
     shots = filters.shape[0]
     channels = gain.shape[0]
@@ -54,6 +56,19 @@
     )
     rank = jnp.sum(jnp.where(hit, running - 1.0, 0.0), axis=0, keepdims=True)
     position = owner_row[...] * capacity + rank.astype(jnp.int32)
+    ranked = jnp.where(iota((128, trace_count), 0) == rank.astype(jnp.int32), 1.0, 0.0)
+    ranked = ranked.astype(jnp.bfloat16)
+
+    def listed(row):
+        named = jnp.where(hit, row.astype(jnp.float32), 0.0).astype(jnp.bfloat16)
+        return lax.dot_general(
+            named, ranked, (((1,), (1,)), ((), ())), preferred_element_type=jnp.float32
+        )
+
+    bin_part = listed(slot_row[...] + 1)
+    codes[:, 0, :] = jnp.where(
+        bin_part > 0, (bin_part - 1) * offsets + listed(class_row[...]) + 1, 0.0
+    )
     slots = owners * capacity
     pick = jnp.where(iota((slots, trace_count), 0) == position, 1.0, 0.0).astype(jnp.bfloat16)
     for lane in range(0, samples, 256):
@@ -62,7 +77,9 @@
         ).astype(jnp.bfloat16)
 
 
-def exchange_kernel(shots, bins, out_ref, in_ref, send_sem, recv_sem, own_sem):
+def exchange_kernel(
+    shots, bins, out_ref, code_out, in_ref, code_in, send_sem, recv_sem, code_send, code_recv, own_sem
+):
     count = shots * bins
     me = lax.axis_index("shot") * bins + lax.axis_index("bin")
     barrier = pltpu.get_barrier_semaphore()
@@ -75,72 +92,77 @@
         return carry
 
     lax.fori_loop(1, count, greet, 0)
-    own = pltpu.make_async_copy(out_ref.at[me], in_ref.at[me], own_sem)
+    own = pltpu.make_async_copy(out_ref.at[me], in_ref.at[me], own_sem.at[0])
     own.start()
+    own_code = pltpu.make_async_copy(code_out.at[me], code_in.at[me], own_sem.at[1])
+    own_code.start()
     pl.semaphore_wait(barrier, count - 1)
 
-    def copy_of(step):
+    def copies_of(step):
         other = lax.rem(me + step, count)
-        return pltpu.make_async_remote_copy(
+        target = (other // bins, lax.rem(other, bins))
+        rows = pltpu.make_async_remote_copy(
             src_ref=out_ref.at[other],
             dst_ref=in_ref.at[me],
             send_sem=send_sem.at[step],
             recv_sem=recv_sem.at[step],
-            device_id=(other // bins, lax.rem(other, bins)),
+            device_id=target,
             device_id_type=MESH,
         )
+        names = pltpu.make_async_remote_copy(
+            src_ref=code_out.at[other],
+            dst_ref=code_in.at[me],
+            send_sem=code_send.at[step],
+            recv_sem=code_recv.at[step],
+            device_id=target,
+            device_id_type=MESH,
+        )
+        return rows, names
 
     def begin(step, carry):
-        copy_of(step).start()
+        for copy in copies_of(step):
+            copy.start()
         return carry
 
     def finish(step, carry):
-        copy_of(step).wait()
+        for copy in copies_of(step):
+            copy.wait()
         return carry
 
     lax.fori_loop(1, count, begin, 0)
     own.wait()
+    own_code.wait()
     lax.fori_loop(1, count, finish, 0)
 
 
-def exchange(outgoing, collective_id):
+def exchange(outgoing, codes, collective_id):
     shots, bins = lax.axis_size("shot"), lax.axis_size("bin")
     count = shots * bins
     return pl.pallas_call(
         functools.partial(exchange_kernel, shots, bins),
-        out_shape=jax.ShapeDtypeStruct(outgoing.shape, outgoing.dtype),
-        in_specs=[pl.BlockSpec(memory_space=pl.ANY)],
-        out_specs=pl.BlockSpec(memory_space=pl.ANY),
-        scratch_shapes=[
-            pltpu.SemaphoreType.DMA((count,)),
-            pltpu.SemaphoreType.DMA((count,)),
-            pltpu.SemaphoreType.DMA,
-        ],
+        out_shape=(
+            jax.ShapeDtypeStruct(outgoing.shape, outgoing.dtype),
+            jax.ShapeDtypeStruct(codes.shape, codes.dtype),
+        ),
+        in_specs=[pl.BlockSpec(memory_space=pltpu.VMEM)] * 2,
+        out_specs=[pl.BlockSpec(memory_space=pltpu.VMEM)] * 2,
+        scratch_shapes=[pltpu.SemaphoreType.DMA((count,)) for _ in range(4)]
+        + [pltpu.SemaphoreType.DMA((2,))],
         compiler_params=pltpu.CompilerParams(
-            collective_id=collective_id, has_side_effects=True
+            collective_id=collective_id, has_side_effects=True, vmem_limit_bytes=VMEM_BYTES
         ),
         name="exchange",
-    )(outgoing)
+    )(outgoing, codes)
 
 
 def bin_kernel(capacity, cells_here, arrived, codes, lo, hi):
-    owners, trace_count = codes.shape
+    owners = codes.shape[0]
     slots, samples = arrived.shape
-    local = codes[...]
-    mine = (local >= 0) & (local < cells_here)
-    upper = iota((trace_count, trace_count), 0) <= iota((trace_count, trace_count), 1)
-    running = jnp.dot(
-        jnp.where(mine, 1.0, 0.0).astype(jnp.bfloat16),
-        jnp.where(upper, 1.0, 0.0).astype(jnp.bfloat16),
-        preferred_element_type=jnp.float32,
-    )
-    ranked = jnp.where(mine, running, 0.0)
-    named = local.astype(jnp.float32) + 1.0
+    listed = codes[:, 0, :]
     place = iota((owners, slots), 1) - capacity * iota((owners, slots), 0)
     spread = jnp.zeros((owners, slots), jnp.float32)
     for rank in range(capacity):
-        code = jnp.sum(jnp.where(ranked == rank + 1.0, named, 0.0), axis=1, keepdims=True)
-        spread = jnp.where(place == rank, code, spread)
+        spread = jnp.where(place == rank, listed[:, rank : rank + 1], spread)
     slot_code = jnp.sum(spread, axis=0, keepdims=True).astype(jnp.int32)
     member_f = jnp.where(iota((cells_here, slots), 0) + 1 == slot_code, 1.0, 0.0)
     fold = jnp.sum(member_f, axis=1, keepdims=True)
@@ -213,23 +235,21 @@
         for first in range(0, offsets, 8):
             group = slice(first, first + 8)
             at = start[group, lanes] - (128 * block - 64)
-            index, early, weight = [], [], []
             for tap in range(nmo_taps):
                 moved = at + tap
-                index.append(moved & 127)
-                early.append(moved < 128)
-                weight.append(weights[tap, group, lanes])
-            for cell in range(IL_DEV * XL_DEV):
-                place = (cell // XL_DEV, cell % XL_DEV // 2, cell % 2)
-                here = filtered[(block,) + place + (group, slice(None))]
-                after = filtered[(block + 1,) + place + (group, slice(None))]
-                for tap in range(nmo_taps):
+                index = moved & 127
+                early = moved < 128
+                weight = weights[tap, group, lanes]
+                for cell in range(IL_DEV * XL_DEV):
+                    place = (cell // XL_DEV, cell % XL_DEV // 2, cell % 2)
+                    here = filtered[(block,) + place + (group, slice(None))]
+                    after = filtered[(block + 1,) + place + (group, slice(None))]
                     value = jnp.where(
-                        early[tap],
-                        jnp.take_along_axis(here, index[tap], axis=1),
-                        jnp.take_along_axis(after, index[tap], axis=1),
+                        early,
+                        jnp.take_along_axis(here, index, axis=1),
+                        jnp.take_along_axis(after, index, axis=1),
                     )
-                    totals[cell] = totals[cell] + value * weight[tap]
+                    totals[cell] = totals[cell] + value * weight
         for inline in range(IL_DEV):
             rows = [
                 jnp.sum(totals[inline * XL_DEV + x], axis=0, keepdims=True) for x in range(XL_DEV)
@@ -253,7 +273,6 @@
 ):
     bins = lax.axis_size("bin")
     owners = lax.axis_size("shot") * bins
-    me = lax.axis_index("shot") * bins + lax.axis_index("bin")
     trace_count, samples = traces.shape
     capacity = 2 * trace_count // owners
     slots = owners * capacity
@@ -264,21 +283,27 @@
     anywhere = pl.BlockSpec(memory_space=pl.ANY)
     params = pltpu.CompilerParams(vmem_limit_bytes=VMEM_BYTES)
 
-    owner = bin_owner[:, 0]
-    code = owner * cells_here + bin_slot * offsets + offset_class
-    codes = lax.all_gather(code, AXES) - me * cells_here
-
-    outgoing = pl.pallas_call(
-        functools.partial(decon_kernel, owners, capacity),
-        out_shape=jax.ShapeDtypeStruct((slots, samples), jnp.bfloat16),
-        in_specs=[vmem] * 4,
-        out_specs=vmem,
+    outgoing, codes = pl.pallas_call(
+        functools.partial(decon_kernel, owners, capacity, offsets),
+        out_shape=(
+            jax.ShapeDtypeStruct((slots, samples), jnp.bfloat16),
+            jax.ShapeDtypeStruct((owners, 1, 128), jnp.float32),
+        ),
+        in_specs=[vmem] * 6,
+        out_specs=(vmem, vmem),
         scratch_shapes=[pltpu.VMEM((trace_count, samples), jnp.bfloat16)],
         compiler_params=params,
         name="decon",
-    )(traces, shot_filter, channel_gain[:, None], owner[None, :])
-
-    arrived = exchange(outgoing.reshape(owners, capacity, samples), 1)
+    )(
+        traces,
+        shot_filter,
+        channel_gain[:, None],
+        bin_owner.reshape(1, trace_count),
+        bin_slot[None, :],
+        offset_class[None, :],
+    )
+
+    arrived, codes = exchange(outgoing.reshape(owners, capacity, samples), codes, 1)
 
     rim = jax.ShapeDtypeStruct((IL_DEV, half, offsets, samples), jnp.bfloat16)
     lo, hi = pl.pallas_call(

time: 189 us -> 124 us (0.66)
  blocking collectives: 31.3 us -> 0 us
  Pallas kernels: 117 us -> 86.6 us
    all_gather x1 -> x0, blocking collectives: 31.3 us -> none  [per_device(): codes = lax.all_gather(code, AXES) - me * cells_here]
    pallas_call x1, Pallas kernels: 52.7 us -> 31.5 us  [per_device(): pl.pallas_call(functools.partial(stack_kernel, taps), out_shape=jax.Shape...]
    pallas_call x1, Pallas kernels: 61.6 us -> 51.6 us  [exchange(): pl.pallas_call(functools.partial(exchange_kernel, shots, bins), out_shape...]
  transfers between devices with their start and end apart: 2 -> 2, of which waited for: 2 -> 2; matrix products, arithmetic and copies ran while one was open for 1% -> 2% of each run, Pallas kernels for 0% -> 0%
where the time goes in v2:
time: 124 us; the launch traced here: 123 us
  Pallas kernels  86.6 us (70%)
  waiting for transfers between devices  21.2 us (17%)
  starting transfers between devices  8.58 us (7%)
  local copies, waits for them, and re-layouts  4.82 us (4%)
  other arithmetic  1.92 us (2%)
    pallas_call x1, Pallas kernels, exchange(): pl.pallas_call(functools.partial(exchange_kernel, shots, bins), out_shape...  51.6 us
    pallas_call x1, Pallas kernels, per_device(): pl.pallas_call(functools.partial(stack_kernel, taps), out_shape=jax.Shape...  31.5 us
    ppermute x1, waiting for transfers between devices, per_device(): left = lax.ppermute(hi, 'bin', [(i, i + 1) for i in range(bins - 1)])  18.1 us
    ppermute x1, starting transfers between devices, per_device(): left = lax.ppermute(hi, 'bin', [(i, i + 1) for i in range(bins - 1)])  6.66 us
    unnamed x14, local copies, waits for them, and re-layouts  3.93 us
    ppermute x1, waiting for transfers between devices, per_device(): right = lax.ppermute(lo, 'bin', [(i + 1, i) for i in range(bins - 1)])  3.07 us
  transfers between devices with their start and end apart: 2, of which 2 were waited for; matrix products, arithmetic and copies ran while one was open for 2% of the time, Pallas kernels for 0%

profile of v2, /device:TPU:11, one launch (start us, length us, event | category | flops | bytes accessed | tf_op | source)
XLA Modules:
  0.0 123.2 jit_solution(15265409138598951425)
XLA Ops:
  0.0 0.8 copy.11.gain
  0.8 0.0 copy-start
  0.8 1.2 copy-done
  2.0 0.0 copy-start.2
  2.0 0.7 copy-done.2
  2.7 0.0 copy-start.3
  2.7 0.7 copy-done.3
  3.4 0.7 copy-done.4
  4.1 0.7 copy-done.5
  4.7 1.5 %decon.1 = (bf16[512,2048]{1,0:T(8,128)(2,1)S(1)}, f32[32,1,128]{2,1,0:T(1,128)S(1)}) custom-call(bf16[256,2048]{1,0:T(8,128)(2,1)S(1)} %copy-done, bf16[1,128]{1,0:T(2,128)(2,1)S(1)} %copy-done.5, f32[256,1]{1,0:T(8,128)S(1)} %copy.11.gain, s32[1,256]{1,0:T(1,128)S(1)} %bitcast.10, s32[1,256]{1,0:T(1,128)S(1)} %bitcast.11, s32[1,256]{1,0:T(1,128)S(1)} %bitcast.12), custom_call_target="tpu_custom_call" | custom-call | tf_op jit(solution)/shard_map/decon/pallas_call | solution.py:286
  6.3 0.0 copy-start.6
  6.3 51.6 %exchange.1 = (bf16[32,16,2048]{2,1,0:T(8,128)(2,1)S(1)}, f32[32,1,128]{2,1,0:T(1,128)S(1)}) custom-call(bf16[32,16,2048]{2,1,0:T(8,128)(2,1)S(1)} %bitcast.9, f32[32,1,128]{2,1,0:T(1,128)S(1)} %get-tuple-element.12.code_out), custom_call_target="tpu_custom_call" | custom-call | tf_op jit(solution)/shard_map/exchange/pallas_call | solution.py:141
  57.9 2.0 %bin.1 = (bf16[2,4,32,2048]{3,2,1,0:T(8,128)(2,1)S(1)}, bf16[2,4,32,2048]{3,2,1,0:T(8,128)(2,1)S(1)}) custom-call(bf16[512,2048]{1,0:T(8,128)(2,1)S(1)} %bitcast.8, f32[32,1,128]{2,1,0:T(1,128)S(1)} %get-tuple-element.14.codes), custom_call_target="tpu_custom_call" | custom-call | tf_op jit(solution)/shard_map/bin/pallas_call | solution.py:309
  59.9 0.0 copy-start.1
  59.9 6.7 %collective-permute-start = (bf16[2,4,32,2048]{3,2,1,0:T(8,128)(2,1)S(1)}, bf16[2,4,32,2048]{3,2,1,0:T(8,128)(2,1)S(1)}, u32[]{:S(2)}, u32[]{:S(2)}) collective-permute-start(bf16[2,4,32,2048]{3,2,1,0:T(8,128)(2,1)S(1)} %get-tuple-element.15.hi), channel_id=1, source_target_pairs={{0,1},{1,2},{2,3},{3,4},{4,5},{5,6},{6,7},{8,9},{9,10},{10,11},{11... | collective-permute-start | bytes 3145736 | tf_op jit(solution)/shard_map/ppermute | solution.py:319
  66.6 1.9 %collective-permute-start.1 = (bf16[2,4,32,2048]{3,2,1,0:T(8,128)(2,1)S(1)}, bf16[2,4,32,2048]{3,2,1,0:T(8,128)(2,1)}, u32[]{:S(2)}, u32[]{:S(2)}) collective-permute-start(bf16[2,4,32,2048]{3,2,1,0:T(8,128)(2,1)S(1)} %get-tuple-element.16.lo), channel_id=1, source_target_pairs={{1,0},{2,1},{3,2},{4,3},{5,4},{6,5},{7,6},{9,8},{10,9},{11,10},{12... | collective-permute-start | bytes 3145736 | tf_op jit(solution)/shard_map/ppermute | solution.py:318
  68.5 0.0 copy-done.6
  68.5 0.1 rev.3
  68.6 0.1 pad_convert_fusion.dip_rows
  68.7 1.8 %convert_bitcast_fusion.weights = f32[8,32,2048]{2,1,0:T(8,128)S(1)} fusion(bf16[32,8,2048]{2,1,0:T(8,128)(2,1)} %param.17), kind=kLoop, calls=%fused_computation | loop fusion | flops 524288 | bytes 3145728 | tf_op jit(solution)/shard_map/convert_element_type | solution.py:327
  70.5 18.1 %collective-permute-done.left = bf16[2,4,32,2048]{3,2,1,0:T(8,128)(2,1)S(1)} collective-permute-done((bf16[2,4,32,2048]{3,2,1,0:T(8,128)(2,1)S(1)}, bf16[2,4,32,2048]{3,2,1,0:T(8,128)(2,1)S(1)}, u32[]{:S(2)}, u32[]{:S(2)}) %collective-permute-start) | collective-permute-done | bytes 1048608 | tf_op jit(solution)/shard_map/ppermute | solution.py:319
  88.6 3.1 %collective-permute-done.1.right = bf16[2,4,32,2048]{3,2,1,0:T(8,128)(2,1)} collective-permute-done((bf16[2,4,32,2048]{3,2,1,0:T(8,128)(2,1)S(1)}, bf16[2,4,32,2048]{3,2,1,0:T(8,128)(2,1)}, u32[]{:S(2)}, u32[]{:S(2)}) %collective-permute-start.1) | collective-permute-done | bytes 1048608 | tf_op jit(solution)/shard_map/ppermute | solution.py:318
  91.7 0.0 copy-done.1
  91.7 31.5 %stack.1 = f32[2,8,2048]{2,1,0:T(8,128)} custom-call(bf16[2,4,32,2048]{3,2,1,0:T(8,128)(2,1)S(1)} %collective-permute-done.left, bf16[2,4,32,2048]{3,2,1,0:T(8,128)(2,1)S(1)} %get-tuple-element.16.lo, bf16[2,4,32,2048]{3,2,1,0:T(8,128)(2,1)S(1)} %get-tuple-element.15.hi, bf16[2,4,32,2048]{3,2,1,0:T(8,128)(2,1)} %collective-permute-done.1.right, ...), custom_call_target="tpu_custom_call" | custom-call | tf_op jit(solution)/shard_map/stack/pallas_call | solution.py:329
  (2 shorter events, 0.0 us)
Async XLA Ops:
  0.8 1.2 copy-start
  2.0 0.7 copy-start.2
  2.7 0.7 copy-start.3
  3.4 0.7 copy-start.4
  4.1 0.7 copy-start.5
  6.3 62.2 %copy-start.6 = (bf16[9,31]{1,0:T(8,128)(2,1)S(1)}, bf16[9,31]{1,0:T(8,128)(2,1)}, u32[]{:S(2)}) copy-start(bf16[9,31]{1,0:T(8,128)(2,1)} %param.15) | copy-start | bytes 1678
  59.9 31.8 %copy-start.1 = (s32[32,2048]{1,0:T(8,128)S(1)}, s32[32,2048]{1,0:T(8,128)}, u32[]{:S(2)}) copy-start(s32[32,2048]{1,0:T(8,128)} %start.1) | copy-start | bytes 786436
  59.9 28.7 %collective-permute-start = (bf16[2,4,32,2048]{3,2,1,0:T(8,128)(2,1)S(1)}, bf16[2,4,32,2048]{3,2,1,0:T(8,128)(2,1)S(1)}, u32[]{:S(2)}, u32[]{:S(2)}) collective-permute-start(bf16[2,4,32,2048]{3,2,1,0:T(8,128)(2,1)S(1)} %get-tuple-element.15.hi), channel_id=1, source_target_pairs={{0,1},{1,2},{2,3},{3,4},{4,5},{5,6},{6,7},{8,9},{9,10},{10,11},{11... | collective-permute-start | bytes 3145736 | tf_op jit(solution)/shard_map/ppermute | solution.py:319
  66.6 25.1 %collective-permute-start.1 = (bf16[2,4,32,2048]{3,2,1,0:T(8,128)(2,1)S(1)}, bf16[2,4,32,2048]{3,2,1,0:T(8,128)(2,1)}, u32[]{:S(2)}, u32[]{:S(2)}) collective-permute-start(bf16[2,4,32,2048]{3,2,1,0:T(8,128)(2,1)S(1)} %get-tuple-element.16.lo), channel_id=1, source_target_pairs={{1,0},{2,1},{3,2},{4,3},{5,4},{6,5},{7,6},{9,8},{10,9},{11,10},{12... | collective-permute-start | bytes 3145736 | tf_op jit(solution)/shard_map/ppermute | solution.py:318

commit v3 on v2

v3 whole, which is shorter than its diff:
```python
import functools
import math

import jax
import jax.numpy as jnp
from jax import lax
from jax.experimental import pallas as pl
from jax.experimental.pallas import tpu as pltpu
from jax.sharding import PartitionSpec as P

IL_DEV = 2
XL_DEV = 8
MESH = pl.DeviceIdType.MESH
AXES = ("shot", "bin")
VMEM_BYTES = 40 * 1024 * 1024


def iota(shape, dim):
    return lax.broadcasted_iota(jnp.int32, shape, dim)


def toeplitz(row):
    return pltpu.roll(jnp.broadcast_to(row, (256, 256)), 0, 1, stride=1, stride_axis=0)


def decon_kernel(
    owners, capacity, offsets, traces_hbm, gain_hbm, owner_hbm, slot_hbm, class_hbm, filters, *rest
):
    outs, (codes, traces, gain, owner_v, slot_v, class_v, dec, sems) = rest[:-8], rest[-8:]
    copies = [
        pltpu.make_async_copy(source, target, sems.at[number])
        for number, (source, target) in enumerate(
            (
                (owner_hbm, owner_v),
                (slot_hbm, slot_v),
                (class_hbm, class_v),
                (gain_hbm, gain),
                (traces_hbm, traces),
            )
        )
    ]
    for copy in copies:
        copy.start()
    trace_count, samples = traces.shape
    shots = filters.shape[0]
    channels = trace_count // shots
    for copy in copies[:4]:
        copy.wait()
    owner_row, slot_row, class_row = owner_v[...], slot_v[...], class_v[...]
    hit = iota((owners, trace_count), 0) == owner_row
    hit_f = jnp.where(hit, 1.0, 0.0)
    upper = iota((trace_count, trace_count), 0) <= iota((trace_count, trace_count), 1)
    running = jnp.dot(
        hit_f.astype(jnp.bfloat16),
        jnp.where(upper, 1.0, 0.0).astype(jnp.bfloat16),
        preferred_element_type=jnp.float32,
    )
    rank = jnp.sum(jnp.where(hit, running - 1.0, 0.0), axis=0, keepdims=True)
    position = owner_row * capacity + rank.astype(jnp.int32)
    ranked = jnp.where(iota((128, trace_count), 0) == rank.astype(jnp.int32), 1.0, 0.0)
    ranked = ranked.astype(jnp.bfloat16)

    def listed(row):
        named = jnp.where(hit, row.astype(jnp.float32), 0.0).astype(jnp.bfloat16)
        return lax.dot_general(
            named, ranked, (((1,), (1,)), ((), ())), preferred_element_type=jnp.float32
        )

    bin_part = listed(slot_row + 1)
    codes[:, 0, :] = jnp.where(
        bin_part > 0, (bin_part - 1) * offsets + listed(class_row) + 1, 0.0
    )
    slots = owners * capacity
    pick = jnp.where(iota((slots, trace_count), 0) == position, 1.0, 0.0).astype(jnp.bfloat16)
    factor = jnp.broadcast_to(gain[...], (128, channels)).T
    copies[4].wait()
    for shot in range(shots):
        taps = filters[shot : shot + 1, :].astype(jnp.float32)
        matrix = toeplitz(jnp.concatenate([jnp.zeros_like(taps), taps], axis=1))[:, :128]
        matrix = matrix.astype(jnp.bfloat16)
        rows = slice(shot * channels, (shot + 1) * channels)
        for block in range(samples // 128):
            lanes = slice(128 * block, 128 * block + 128)
            if block == 0:
                product = jnp.dot(
                    traces[rows, lanes], matrix[128:], preferred_element_type=jnp.float32
                )
            else:
                window = slice(128 * block - 128, 128 * block + 128)
                product = jnp.dot(
                    traces[rows, window], matrix, preferred_element_type=jnp.float32
                )
            dec[rows, lanes] = (product * factor).astype(jnp.bfloat16)
    span = samples // len(outs)
    for part, out in enumerate(outs):
        for lane in range(0, span, 256):
            place = part * span + lane
            out[:, lane : lane + 256] = jnp.dot(
                pick, dec[:, place : place + 256], preferred_element_type=jnp.float32
            ).astype(jnp.bfloat16)


def exchange_kernel(shots, bins, arrays, *refs):
    sources, targets = refs[:arrays], refs[arrays : 2 * arrays]
    send_sems = refs[2 * arrays : 3 * arrays]
    recv_sems = refs[3 * arrays : 4 * arrays]
    own_sem = refs[4 * arrays]
    count = shots * bins
    me = lax.axis_index("shot") * bins + lax.axis_index("bin")
    barrier = pltpu.get_barrier_semaphore()

    def greet(step, carry):
        other = lax.rem(me + step, count)
        pl.semaphore_signal(
            barrier, inc=1, device_id=(other // bins, lax.rem(other, bins)), device_id_type=MESH
        )
        return carry

    lax.fori_loop(1, count, greet, 0)
    own = [
        pltpu.make_async_copy(sources[k].at[me], targets[k].at[me], own_sem.at[k])
        for k in range(arrays)
    ]
    for copy in own:
        copy.start()
    pl.semaphore_wait(barrier, count - 1)

    def copies_of(step):
        other = lax.rem(me + step, count)
        return [
            pltpu.make_async_remote_copy(
                src_ref=sources[k].at[other],
                dst_ref=targets[k].at[me],
                send_sem=send_sems[k].at[step],
                recv_sem=recv_sems[k].at[step],
                device_id=(other // bins, lax.rem(other, bins)),
                device_id_type=MESH,
            )
            for k in range(arrays)
        ]

    def begin(step, carry):
        for copy in copies_of(step):
            copy.start()
        return carry

    def finish(step, carry):
        for copy in copies_of(step):
            copy.wait()
        return carry

    lax.fori_loop(1, count, begin, 0)
    for copy in own:
        copy.wait()
    lax.fori_loop(1, count, finish, 0)


def exchange(arrays, collective_id):
    shots, bins = lax.axis_size("shot"), lax.axis_size("bin")
    count = shots * bins
    number = len(arrays)
    return pl.pallas_call(
        functools.partial(exchange_kernel, shots, bins, number),
        out_shape=[jax.ShapeDtypeStruct(array.shape, array.dtype) for array in arrays],
        in_specs=[pl.BlockSpec(memory_space=pltpu.VMEM)] * number,
        out_specs=[pl.BlockSpec(memory_space=pltpu.VMEM)] * number,
        scratch_shapes=[pltpu.SemaphoreType.DMA((count,)) for _ in range(2 * number)]
        + [pltpu.SemaphoreType.DMA((number,))],
        compiler_params=pltpu.CompilerParams(
            collective_id=collective_id, has_side_effects=True, vmem_limit_bytes=VMEM_BYTES
        ),
        name=f"exchange_{collective_id}",
    )(*arrays)


def bin_kernel(capacity, cells_here, arrived, codes, lo, hi):
    owners = codes.shape[0]
    slots, samples = arrived.shape
    listed = codes[:, 0, :]
    place = iota((owners, slots), 1) - capacity * iota((owners, slots), 0)
    spread = jnp.zeros((owners, slots), jnp.float32)
    for rank in range(capacity):
        spread = jnp.where(place == rank, listed[:, rank : rank + 1], spread)
    slot_code = jnp.sum(spread, axis=0, keepdims=True).astype(jnp.int32)
    member_f = jnp.where(iota((cells_here, slots), 0) + 1 == slot_code, 1.0, 0.0)
    fold = jnp.sum(member_f, axis=1, keepdims=True)
    scale = 1.0 / jnp.maximum(fold, 1.0)
    member = member_f.astype(jnp.bfloat16)
    offsets = lo.shape[2]
    half = XL_DEV // 2
    for lane in range(0, samples, 256):
        summed = jnp.dot(
            member, arrived[:, lane : lane + 256], preferred_element_type=jnp.float32
        )
        binned = (summed * scale).astype(jnp.bfloat16).reshape(IL_DEV, XL_DEV, offsets, 256)
        lo[:, :, :, lane : lane + 256] = binned[:, :half]
        hi[:, :, :, lane : lane + 256] = binned[:, half:]


def stack_kernel(taps, first_block, halves, *refs):
    inputs = refs[: 4 * len(halves)]
    rest = refs[4 * len(halves) :]
    earlier = rest[0] if first_block else None
    dip_rows, start, weights, out, ext, matrix, ring, staged, sems = rest[1 if first_block else 0 :]
    crosslines, offsets = ext.shape[1], ext.shape[2]
    blocks = ext.shape[3] // 128 - 2
    half = crosslines // 4
    pairs = XL_DEV // 2
    copies = []
    for number, (source_lane, target_lane, span) in enumerate(halves):
        for part in range(4):
            copy = pltpu.make_async_copy(
                inputs[4 * number + part].at[:, :, :, source_lane : source_lane + span],
                ext.at[:, part * half : part * half + half, :, target_lane : target_lane + span],
                sems.at[4 * number + part],
            )
            copy.start()
            copies.append(copy)
    filled_from = min(target for _, target, _ in halves)
    filled_to = max(target + span for _, target, span in halves)
    for low, high in ((0, filled_from), (filled_to, ext.shape[3])):
        if high > low:
            ext[:, :, :, low:high] = jnp.zeros(
                (IL_DEV, crosslines, offsets, high - low), jnp.bfloat16
            )
    matrix[:256, 128:] = jnp.zeros((256, 128), jnp.bfloat16)
    matrix[256 * taps :, :128] = jnp.zeros((256, 128), jnp.bfloat16)
    for tap in range(taps):
        one = toeplitz(dip_rows[tap : tap + 1, :])[:, :128].astype(jnp.bfloat16)
        matrix[256 * tap : 256 * tap + 256, :128] = one
        matrix[256 * tap + 256 : 256 * tap + 512, 128:] = one
    if first_block:
        out[:, :, : 128 * first_block] = earlier[...]
    for copy in copies:
        copy.wait()

    def filter_block(block, target):
        lanes = pl.ds(pl.multiple_of(128 * block, 128), 256)
        window = ext[:, :, :, lanes].reshape(IL_DEV, crosslines // 2, 2, offsets, 256)
        pieces = []
        for tap in range(taps + 1):
            piece = window[:, tap // 2 : tap // 2 + pairs, tap % 2]
            pieces.append(piece.reshape(IL_DEV * pairs * offsets, 256))
        result = jnp.dot(
            jnp.concatenate(pieces, axis=1), matrix[...], preferred_element_type=jnp.float32
        )
        rounded = result.astype(jnp.bfloat16).astype(jnp.float32)
        for side in range(2):
            target[:, :, side] = rounded[:, 128 * side : 128 * side + 128].reshape(
                IL_DEV, pairs, offsets, 128
            )

    filter_block(0, ring.at[0])
    filter_block(1, ring.at[1])
    nmo_taps = weights.shape[0]
    scale = 1.0 / math.sqrt(offsets)

    def stack_block(block, carry):
        filter_block(jnp.minimum(block + 2, blocks), staged)
        this, following = lax.rem(block, 3), lax.rem(block + 1, 3)
        lanes = pl.ds(pl.multiple_of(128 * (block + first_block), 128), 128)
        totals = [jnp.zeros((8, 128), jnp.float32) for _ in range(IL_DEV * XL_DEV)]
        for first in range(0, offsets, 8):
            group = slice(first, first + 8)
            at = start[group, lanes] - (128 * (block + first_block) - 64)
            for tap in range(nmo_taps):
                moved = at + tap
                index = moved & 127
                early = moved < 128
                weight = weights[tap, group, lanes]
                for cell in range(IL_DEV * XL_DEV):
                    place = (cell // XL_DEV, cell % XL_DEV // 2, cell % 2)
                    here = ring[(this,) + place + (group, slice(None))]
                    after = ring[(following,) + place + (group, slice(None))]
                    value = jnp.where(
                        early,
                        jnp.take_along_axis(here, index, axis=1),
                        jnp.take_along_axis(after, index, axis=1),
                    )
                    totals[cell] = totals[cell] + value * weight
        for inline in range(IL_DEV):
            rows = [
                jnp.sum(totals[inline * XL_DEV + x], axis=0, keepdims=True) for x in range(XL_DEV)
            ]
            out[inline, :, lanes] = jnp.concatenate(rows, axis=0) * scale
        ring[lax.rem(block + 2, 3)] = staged[...]
        return carry

    lax.fori_loop(0, blocks, stack_block, 0)


def per_device(
    traces,
    shot_filter,
    channel_gain,
    bin_owner,
    bin_slot,
    offset_class,
    dip_filter,
    nmo_start,
    nmo_weights,
):
    bins = lax.axis_size("bin")
    owners = lax.axis_size("shot") * bins
    trace_count, samples = traces.shape
    capacity = 2 * trace_count // owners
    slots = owners * capacity
    offsets = nmo_start.shape[0]
    cells_here = IL_DEV * XL_DEV * offsets
    half = XL_DEV // 2
    vmem = pl.BlockSpec(memory_space=pltpu.VMEM)
    anywhere = pl.BlockSpec(memory_space=pl.ANY)
    params = pltpu.CompilerParams(vmem_limit_bytes=VMEM_BYTES)

    parts = 2
    span = samples // parts
    row = jax.ShapeDtypeStruct((slots, span), jnp.bfloat16)
    line = pltpu.VMEM((1, trace_count), jnp.int32)
    *outgoing, codes = pl.pallas_call(
        functools.partial(decon_kernel, owners, capacity, offsets),
        out_shape=[row] * parts + [jax.ShapeDtypeStruct((owners, 1, 128), jnp.float32)],
        in_specs=[pl.BlockSpec(memory_space=pltpu.HBM)] * 5 + [vmem],
        out_specs=[vmem] * (parts + 1),
        scratch_shapes=[
            pltpu.VMEM(traces.shape, jnp.bfloat16),
            pltpu.VMEM((1, channel_gain.shape[0]), jnp.float32),
            line,
            line,
            line,
            pltpu.VMEM(traces.shape, jnp.bfloat16),
            pltpu.SemaphoreType.DMA((5,)),
        ],
        compiler_params=params,
        name="decon",
    )(
        traces,
        channel_gain[None, :],
        bin_owner.reshape(1, trace_count),
        bin_slot[None, :],
        offset_class[None, :],
        shot_filter,
    )

    taps, time_taps = dip_filter.shape
    before = 192 + time_taps // 2 - (time_taps - 1)
    dip_rows = jnp.pad(
        dip_filter[:, ::-1].astype(jnp.float32),
        ((0, 0), (before, 256 - before - time_taps)),
    )
    weights = jnp.transpose(nmo_weights, (1, 0, 2)).astype(jnp.float32)
    crosslines = 2 * XL_DEV

    rim = jax.ShapeDtypeStruct((IL_DEV, half, offsets, span), jnp.bfloat16)
    sides = []
    for part in range(parts):
        rows = outgoing[part].reshape(owners, capacity, span)
        if part == 0:
            arrived, codes = exchange([rows, codes], 1)
        else:
            (arrived,) = exchange([rows], 1 + part)
        lo, hi = pl.pallas_call(
            functools.partial(bin_kernel, capacity, cells_here),
            out_shape=(rim, rim),
            in_specs=[vmem] * 2,
            out_specs=(vmem, vmem),
            compiler_params=params,
            name=f"bin_{part}",
        )(arrived.reshape(slots, span), codes)
        right = lax.ppermute(lo, "bin", [(i + 1, i) for i in range(bins - 1)])
        left = lax.ppermute(hi, "bin", [(i, i + 1) for i in range(bins - 1)])
        sides.append((left, lo, hi, right))

    per_part = span // 128
    total = samples // 128
    stacked = None
    for part in range(parts):
        first = max(per_part * part - 1, 0)
        last = per_part * (part + 1) - 1 if part < parts - 1 else total
        blocks = last - first
        low = first - 1
        operands, halves = [], []
        for piece in range(parts):
            begin = max(low, per_part * piece)
            end = min(last + 1, per_part * (piece + 1))
            if begin < end and piece <= part:
                operands += sides[piece]
                halves.append(
                    (128 * (begin - per_part * piece), 128 * (begin - low), 128 * (end - begin))
                )
        stacked = pl.pallas_call(
            functools.partial(stack_kernel, taps, first, halves),
            out_shape=jax.ShapeDtypeStruct((IL_DEV, XL_DEV, 128 * last), jnp.float32),
            in_specs=[anywhere] * len(operands) + [vmem] * (4 if first else 3),
            out_specs=vmem,
            scratch_shapes=[
                pltpu.VMEM((IL_DEV, crosslines, offsets, 128 * (blocks + 2)), jnp.bfloat16),
                pltpu.VMEM(((taps + 1) * 256, 256), jnp.bfloat16),
                pltpu.VMEM((3, IL_DEV, XL_DEV // 2, 2, offsets, 128), jnp.float32),
                pltpu.VMEM((IL_DEV, XL_DEV // 2, 2, offsets, 128), jnp.float32),
                pltpu.SemaphoreType.DMA((4 * len(halves),)),
            ],
            compiler_params=params,
            name=f"stack_{part}",
        )(*operands, *([stacked] if first else []), dip_rows, nmo_start, weights)
    return stacked


def solution(mesh):
    placed = (
        P(AXES, None),
        P(AXES, None),
        P(),
        P(AXES, None),
        P(AXES),
        P(AXES),
        P(),
        P(),
        P(),
    )
    return jax.shard_map(
        per_device, mesh=mesh, in_specs=placed, out_specs=P("shot", "bin", None), check_vma=False
    )
```

time: 124 us -> 108 us (0.87)
  waiting for transfers between devices: 21.2 us -> 0.1 us
  starting transfers between devices: 8.58 us -> 12.8 us
    ppermute x1 -> x2, waiting for transfers between devices: 18.1 us -> 0.01 us  [per_device(): left = lax.ppermute(hi, 'bin', [(i, i + 1) for i in range(bins - 1)])]
    ppermute x1 -> x2, waiting for transfers between devices: 3.07 us -> 0.09 us  [per_device(): right = lax.ppermute(lo, 'bin', [(i + 1, i) for i in range(bins - 1)])]
    ppermute x1 -> x2, starting transfers between devices: 6.66 us -> 8.97 us  [per_device(): left = lax.ppermute(hi, 'bin', [(i, i + 1) for i in range(bins - 1)])]
    ppermute x1 -> x2, starting transfers between devices: 1.92 us -> 3.84 us  [per_device(): right = lax.ppermute(lo, 'bin', [(i + 1, i) for i in range(bins - 1)])]
    pallas_call x1 -> x2, Pallas kernels: 2.01 us -> 2.9 us  [per_device(): pl.pallas_call(functools.partial(bin_kernel, capacity, cells_here), out_s...]
    pallas_call x2 -> x4, Pallas kernels: 83 us -> 82.2 us  [the longest x2 57 us: exchange(): pl.pallas_call(functools.partial(exchange_kernel, shots, bins, number), o...]
    unnamed x14 -> x16, local copies, waits for them, and re-layouts: 3.93 us -> 4.61 us
  transfers between devices with their start and end apart: 2 -> 4, of which waited for: 2 -> 1; matrix products, arithmetic and copies ran while one was open for 2% -> 2% of each run, Pallas kernels for 0% -> 38%
where the time goes in v3:
time: 108 us; the launch traced here: 107 us
  Pallas kernels  86.9 us (80%)
  starting transfers between devices  12.8 us (12%)
  local copies, waits for them, and re-layouts  4.69 us (4%)
  other arithmetic  1.92 us (2%)
    pallas_call x2, Pallas kernels, exchange(): pl.pallas_call(functools.partial(exchange_kernel, shots, bins, number), o...  57 us
    pallas_call x2, Pallas kernels, per_device(): pl.pallas_call(functools.partial(stack_kernel, taps, first, halves), out_...  25.2 us
    ppermute x2, starting transfers between devices, per_device(): left = lax.ppermute(hi, 'bin', [(i, i + 1) for i in range(bins - 1)])  8.97 us
    unnamed x16, local copies, waits for them, and re-layouts  4.61 us
    ppermute x2, starting transfers between devices, per_device(): right = lax.ppermute(lo, 'bin', [(i + 1, i) for i in range(bins - 1)])  3.84 us
    pallas_call x2, Pallas kernels, per_device(): pl.pallas_call(functools.partial(bin_kernel, capacity, cells_here), out_s...  2.9 us
  transfers between devices with their start and end apart: 4, of which 1 were waited for; matrix products, arithmetic and copies ran while one was open for 2% of the time, Pallas kernels for 38%

profile of v3, /device:TPU:11, one launch (start us, length us, event | category | flops | bytes accessed | tf_op | source)
XLA Modules:
  0.0 106.6 jit_solution(6849144957878559109)
XLA Ops:
  0.0 1.2 %copy-done.1 = bf16[256,2048]{1,0:T(8,128)(2,1)S(1)} copy-done((bf16[256,2048]{1,0:T(8,128)(2,1)S(1)}, bf16[256,2048]{1,0:T(8,128)(2,1)}, u32[]{:S(2)}) %copy-start.1) | copy-done | bytes 1048600
  1.2 0.7 copy-done.2
  1.9 0.7 copy-done.3
  2.6 0.7 copy-done.4
  3.3 0.7 copy-done.5
  3.9 0.7 copy-done.6
  4.6 1.8 %decon.1 = (bf16[512,1024]{1,0:T(8,128)(2,1)S(1)}, bf16[512,1024]{1,0:T(8,128)(2,1)S(1)}, f32[32,1,128]{2,1,0:T(1,128)S(1)}) custom-call(bf16[256,2048]{1,0:T(8,128)(2,1)S(1)} %copy-done.1, f32[1,256]{1,0:T(1,128)S(1)} %bitcast.14, s32[1,256]{1,0:T(1,128)S(1)} %bitcast.15, s32[1,256]{1,0:T(1,128)S(1)} %bitcast.16, s32[1,256]{1,0:T(1,128)S(1)} %bitcast.17, ...), custom_call_target="tpu_custom_call" | custom-call | tf_op jit(solution)/shard_map/decon/pallas_call | solution.py:319
  6.4 28.5 %exchange_1.1 = (bf16[32,16,1024]{2,1,0:T(8,128)(2,1)S(1)}, f32[32,1,128]{2,1,0:T(1,128)S(1)}) custom-call(bf16[32,16,1024]{2,1,0:T(8,128)(2,1)S(1)} %bitcast.13, f32[32,1,128]{2,1,0:T(1,128)S(1)} %get-tuple-element.15.refs_1_), custom_call_target="tpu_custom_call" | custom-call | tf_op jit(solution)/shard_map/exchange_1/pallas_call | solution.py:162
  34.9 0.0 copy-start.7
  34.9 1.4 %bin_0.1 = (bf16[2,4,32,1024]{3,2,1,0:T(8,128)(2,1)S(1)}, bf16[2,4,32,1024]{3,2,1,0:T(8,128)(2,1)S(1)}) custom-call(bf16[512,1024]{1,0:T(8,128)(2,1)S(1)} %bitcast.12, f32[32,1,128]{2,1,0:T(1,128)S(1)} %get-tuple-element.17.codes), custom_call_target="tpu_custom_call" | custom-call | tf_op jit(solution)/shard_map/bin_0/pallas_call | solution.py:361
  36.4 4.6 %collective-permute-start = (bf16[2,4,32,1024]{3,2,1,0:T(8,128)(2,1)S(1)}, bf16[2,4,32,1024]{3,2,1,0:T(8,128)(2,1)S(1)}, u32[]{:S(2)}, u32[]{:S(2)}) collective-permute-start(bf16[2,4,32,1024]{3,2,1,0:T(8,128)(2,1)S(1)} %get-tuple-element.18.refs_2_), channel_id=1, source_target_pairs={{0,1},{1,2},{2,3},{3,4},{4,5},{5,6},{6,7},{8,9},{9,10},{10,11},{11... | collective-permute-start | bytes 1572872 | tf_op jit(solution)/shard_map/ppermute | solution.py:370
  41.0 1.9 %collective-permute-start.1 = (bf16[2,4,32,1024]{3,2,1,0:T(8,128)(2,1)S(1)}, bf16[2,4,32,1024]{3,2,1,0:T(8,128)(2,1)S(1)}, u32[]{:S(2)}, u32[]{:S(2)}) collective-permute-start(bf16[2,4,32,1024]{3,2,1,0:T(8,128)(2,1)S(1)} %get-tuple-element.19.refs_1_), channel_id=1, source_target_pairs={{1,0},{2,1},{3,2},{4,3},{5,4},{6,5},{7,6},{9,8},{10,9},{11,10},{12... | collective-permute-start | bytes 1572872 | tf_op jit(solution)/shard_map/ppermute | solution.py:369
  42.9 28.5 %exchange_2.1 = bf16[32,16,1024]{2,1,0:T(8,128)(2,1)S(1)} custom-call(bf16[32,16,1024]{2,1,0:T(8,128)(2,1)S(1)} %bitcast.11), custom_call_target="tpu_custom_call" | custom-call | tf_op jit(solution)/shard_map/exchange_2/pallas_call | solution.py:162
  71.4 0.0 copy-start
  71.4 1.5 %bin_1.1 = (bf16[2,4,32,1024]{3,2,1,0:T(8,128)(2,1)S(1)}, bf16[2,4,32,1024]{3,2,1,0:T(8,128)(2,1)S(1)}) custom-call(bf16[512,1024]{1,0:T(8,128)(2,1)S(1)} %bitcast.10, f32[32,1,128]{2,1,0:T(1,128)S(1)} %get-tuple-element.17.codes), custom_call_target="tpu_custom_call" | custom-call | tf_op jit(solution)/shard_map/bin_1/pallas_call | solution.py:361
  72.9 4.4 %collective-permute-start.2 = (bf16[2,4,32,1024]{3,2,1,0:T(8,128)(2,1)S(1)}, bf16[2,4,32,1024]{3,2,1,0:T(8,128)(2,1)}, u32[]{:S(2)}, u32[]{:S(2)}) collective-permute-start(bf16[2,4,32,1024]{3,2,1,0:T(8,128)(2,1)S(1)} %get-tuple-element.21.refs_6_), channel_id=1, source_target_pairs={{0,1},{1,2},{2,3},{3,4},{4,5},{5,6},{6,7},{8,9},{9,10},{10,11},{11... | collective-permute-start | bytes 1572872 | tf_op jit(solution)/shard_map/ppermute | solution.py:370
  77.3 1.9 %collective-permute-start.3 = (bf16[2,4,32,1024]{3,2,1,0:T(8,128)(2,1)S(1)}, bf16[2,4,32,1024]{3,2,1,0:T(8,128)(2,1)}, u32[]{:S(2)}, u32[]{:S(2)}) collective-permute-start(bf16[2,4,32,1024]{3,2,1,0:T(8,128)(2,1)S(1)} %get-tuple-element.22.refs_5_), channel_id=1, source_target_pairs={{1,0},{2,1},{3,2},{4,3},{5,4},{6,5},{7,6},{9,8},{10,9},{11,10},{12... | collective-permute-start | bytes 1572872 | tf_op jit(solution)/shard_map/ppermute | solution.py:369
  79.2 0.1 rev.3
  79.3 0.1 pad_convert_fusion.refs_4_.refs_9_
  79.4 1.8 %convert_bitcast_fusion.refs_6_.refs_11_ = f32[8,32,2048]{2,1,0:T(8,128)S(1)} fusion(bf16[32,8,2048]{2,1,0:T(8,128)(2,1)} %param.17), kind=kLoop, calls=%fused_computation | loop fusion | flops 524288 | bytes 3145728 | tf_op jit(solution)/shard_map/convert_element_type | solution.py:350
  81.2 0.0 collective-permute-done.refs_0_
  81.2 10.5 %stack_0.1.refs_8_ = f32[2,8,896]{2,1,0:T(8,128)S(1)} custom-call(bf16[2,4,32,1024]{3,2,1,0:T(8,128)(2,1)S(1)} %collective-permute-done.refs_0_, bf16[2,4,32,1024]{3,2,1,0:T(8,128)(2,1)S(1)} %get-tuple-element.19.refs_1_, bf16[2,4,32,1024]{3,2,1,0:T(8,128)(2,1)S(1)} %get-tuple-element.18.refs_2_, ...), custom_call_target="tpu_custom_call" | custom-call | tf_op jit(solution)/shard_map/stack_0/pallas_call | solution.py:390
  91.8 0.1 collective-permute-done.3.refs_7_
  91.9 14.7 %stack_1.1 = f32[2,8,2048]{2,1,0:T(8,128)} custom-call(bf16[2,4,32,1024]{3,2,1,0:T(8,128)(2,1)S(1)} %collective-permute-done.refs_0_, bf16[2,4,32,1024]{3,2,1,0:T(8,128)(2,1)S(1)} %get-tuple-element.19.refs_1_, bf16[2,4,32,1024]{3,2,1,0:T(8,128)(2,1)S(1)} %get-tuple-element.18.refs_2_, bf16[2,4,32,1024]{3,2,1,0:T(8,128)(2,1)S(1)} %collective-permute-done.1.refs_3_, ...), custom_call_target="tpu_custom_call" | custom-call | tf_op jit(solution)/shard_map/stack_1/pallas_call | solution.py:390
  (10 shorter events, 0.0 us)
Async XLA Ops:
  0.0 1.2 %copy-start.1 = (bf16[256,2048]{1,0:T(8,128)(2,1)S(1)}, bf16[256,2048]{1,0:T(8,128)(2,1)}, u32[]{:S(2)}) copy-start(bf16[256,2048]{1,0:T(8,128)(2,1)} %traces_hbm.1) | copy-start | bytes 3145732
  1.2 0.7 copy-start.2
  1.9 0.7 copy-start.3
  2.6 0.7 copy-start.4
  3.3 0.7 copy-start.5
  3.9 0.7 copy-start.6
  34.9 44.3 %copy-start.7 = (bf16[9,31]{1,0:T(8,128)(2,1)S(1)}, bf16[9,31]{1,0:T(8,128)(2,1)}, u32[]{:S(2)}) copy-start(bf16[9,31]{1,0:T(8,128)(2,1)} %param.15) | copy-start | bytes 1678
  36.4 44.8 %collective-permute-start = (bf16[2,4,32,1024]{3,2,1,0:T(8,128)(2,1)S(1)}, bf16[2,4,32,1024]{3,2,1,0:T(8,128)(2,1)S(1)}, u32[]{:S(2)}, u32[]{:S(2)}) collective-permute-start(bf16[2,4,32,1024]{3,2,1,0:T(8,128)(2,1)S(1)} %get-tuple-element.18.refs_2_), channel_id=1, source_target_pairs={{0,1},{1,2},{2,3},{3,4},{4,5},{5,6},{6,7},{8,9},{9,10},{10,11},{11... | collective-permute-start | bytes 1572872 | tf_op jit(solution)/shard_map/ppermute | solution.py:370
  41.0 40.3 %collective-permute-start.1 = (bf16[2,4,32,1024]{3,2,1,0:T(8,128)(2,1)S(1)}, bf16[2,4,32,1024]{3,2,1,0:T(8,128)(2,1)S(1)}, u32[]{:S(2)}, u32[]{:S(2)}) collective-permute-start(bf16[2,4,32,1024]{3,2,1,0:T(8,128)(2,1)S(1)} %get-tuple-element.19.refs_1_), channel_id=1, source_target_pairs={{1,0},{2,1},{3,2},{4,3},{5,4},{6,5},{7,6},{9,8},{10,9},{11,10},{12... | collective-permute-start | bytes 1572872 | tf_op jit(solution)/shard_map/ppermute | solution.py:369
  71.4 9.8 %copy-start = (s32[32,2048]{1,0:T(8,128)S(1)}, s32[32,2048]{1,0:T(8,128)}, u32[]{:S(2)}) copy-start(s32[32,2048]{1,0:T(8,128)} %refs_10_.1) | copy-start | bytes 786436
  72.9 18.9 %collective-permute-start.2 = (bf16[2,4,32,1024]{3,2,1,0:T(8,128)(2,1)S(1)}, bf16[2,4,32,1024]{3,2,1,0:T(8,128)(2,1)}, u32[]{:S(2)}, u32[]{:S(2)}) collective-permute-start(bf16[2,4,32,1024]{3,2,1,0:T(8,128)(2,1)S(1)} %get-tuple-element.21.refs_6_), channel_id=1, source_target_pairs={{0,1},{1,2},{2,3},{3,4},{4,5},{5,6},{6,7},{8,9},{9,10},{10,11},{11... | collective-permute-start | bytes 1572872 | tf_op jit(solution)/shard_map/ppermute | solution.py:370
  77.3 14.6 %collective-permute-start.3 = (bf16[2,4,32,1024]{3,2,1,0:T(8,128)(2,1)S(1)}, bf16[2,4,32,1024]{3,2,1,0:T(8,128)(2,1)}, u32[]{:S(2)}, u32[]{:S(2)}) collective-permute-start(bf16[2,4,32,1024]{3,2,1,0:T(8,128)(2,1)S(1)} %get-tuple-element.22.refs_5_), channel_id=1, source_target_pairs={{1,0},{2,1},{3,2},{4,3},{5,4},{6,5},{7,6},{9,8},{10,9},{11,10},{12... | collective-permute-start | bytes 1572872 | tf_op jit(solution)/shard_map/ppermute | solution.py:369

commit v4 on v3

--- a/solution.py
+++ b/solution.py
@@ -23,30 +23,13 @@
     return pltpu.roll(jnp.broadcast_to(row, (256, 256)), 0, 1, stride=1, stride_axis=0)
 
 
-def decon_kernel(
-    owners, capacity, offsets, traces_hbm, gain_hbm, owner_hbm, slot_hbm, class_hbm, filters, *rest
-):
-    outs, (codes, traces, gain, owner_v, slot_v, class_v, dec, sems) = rest[:-8], rest[-8:]
-    copies = [
-        pltpu.make_async_copy(source, target, sems.at[number])
-        for number, (source, target) in enumerate(
-            (
-                (owner_hbm, owner_v),
-                (slot_hbm, slot_v),
-                (class_hbm, class_v),
-                (gain_hbm, gain),
-                (traces_hbm, traces),
-            )
-        )
-    ]
-    for copy in copies:
-        copy.start()
+def decon_kernel(owners, capacity, offsets, shots, traces, table, *rest):
+    outs, (codes, dec) = rest[:-2], rest[-2:]
     trace_count, samples = traces.shape
-    shots = filters.shape[0]
     channels = trace_count // shots
-    for copy in copies[:4]:
-        copy.wait()
-    owner_row, slot_row, class_row = owner_v[...], slot_v[...], class_v[...]
+    owner_row, slot_row, class_row = (
+        table[row : row + 1, :trace_count].astype(jnp.int32) for row in range(3)
+    )
     hit = iota((owners, trace_count), 0) == owner_row
     hit_f = jnp.where(hit, 1.0, 0.0)
     upper = iota((trace_count, trace_count), 0) <= iota((trace_count, trace_count), 1)
@@ -72,11 +55,9 @@
     )
     slots = owners * capacity
     pick = jnp.where(iota((slots, trace_count), 0) == position, 1.0, 0.0).astype(jnp.bfloat16)
-    factor = jnp.broadcast_to(gain[...], (128, channels)).T
-    copies[4].wait()
+    factor = jnp.broadcast_to(table[3:4, :channels], (128, channels)).T
     for shot in range(shots):
-        taps = filters[shot : shot + 1, :].astype(jnp.float32)
-        matrix = toeplitz(jnp.concatenate([jnp.zeros_like(taps), taps], axis=1))[:, :128]
+        matrix = toeplitz(table[4 + shot : 5 + shot, :256])[:, :128]
         matrix = matrix.astype(jnp.bfloat16)
         rows = slice(shot * channels, (shot + 1) * channels)
         for block in range(samples // 128):
@@ -100,13 +81,25 @@
             ).astype(jnp.bfloat16)
 
 
-def exchange_kernel(shots, bins, arrays, *refs):
-    sources, targets = refs[:arrays], refs[arrays : 2 * arrays]
-    send_sems = refs[2 * arrays : 3 * arrays]
-    recv_sems = refs[3 * arrays : 4 * arrays]
-    own_sem = refs[4 * arrays]
+def exchange_kernel(shots, bins, arrays, halo, prepare, *refs):
     count = shots * bins
-    me = lax.axis_index("shot") * bins + lax.axis_index("bin")
+    refs = list(refs)
+
+    def take(number):
+        taken = refs[:number]
+        del refs[:number]
+        return taken
+
+    sources = take(arrays)
+    tables = take(2) if prepare else None
+    lo, hi = take(2) if halo else (None, None)
+    targets = take(arrays)
+    results = take(2) if prepare else None
+    left, right = take(2) if halo else (None, None)
+    send_sems, recv_sems = take(arrays), take(arrays)
+    own_sem, halo_sem = refs
+    here, bin_here = lax.axis_index("shot"), lax.axis_index("bin")
+    me = here * bins + bin_here
     barrier = pltpu.get_barrier_semaphore()
 
     def greet(step, carry):
@@ -125,52 +118,136 @@
         copy.start()
     pl.semaphore_wait(barrier, count - 1)
 
-    def copies_of(step):
-        other = lax.rem(me + step, count)
+    def copies_of(shot_step, bin_step):
+        shot = lax.rem(here + shot_step, shots)
+        crossline = lax.rem(bin_here + bin_step, bins)
+        other = shot * bins + crossline
         return [
             pltpu.make_async_remote_copy(
                 src_ref=sources[k].at[other],
                 dst_ref=targets[k].at[me],
-                send_sem=send_sems[k].at[step],
-                recv_sem=recv_sems[k].at[step],
-                device_id=(other // bins, lax.rem(other, bins)),
+                send_sem=send_sems[k].at[shot_step * bins + bin_step],
+                recv_sem=recv_sems[k].at[shot_step * bins + bin_step],
+                device_id=(shot, crossline),
                 device_id_type=MESH,
             )
             for k in range(arrays)
         ]
 
-    def begin(step, carry):
-        for copy in copies_of(step):
-            copy.start()
-        return carry
-
-    def finish(step, carry):
-        for copy in copies_of(step):
-            copy.wait()
-        return carry
-
-    lax.fori_loop(1, count, begin, 0)
+    far_first = sorted(range(1, shots), key=lambda step: -min(step, shots - step))
+
+    def each(action):
+        def one(bin_step, carry):
+            for shot_step in far_first:
+                for copy in copies_of(shot_step, bin_step):
+                    action(copy)
+
+            @pl.when(bin_step > 0)
+            def _():
+                for copy in copies_of(0, bin_step):
+                    action(copy)
+
+            return carry
+
+        return one
+
+    def rim_copy(source, target, sem, step):
+        return pltpu.make_async_remote_copy(
+            src_ref=source,
+            dst_ref=target,
+            send_sem=halo_sem.at[sem],
+            recv_sem=halo_sem.at[sem + 1],
+            device_id=(here, bin_here + step),
+            device_id_type=MESH,
+        )
+
+    begin = each(lambda copy: copy.start())
+    lax.fori_loop(0, bins // 2, begin, 0)
+    if halo:
+
+        @pl.when(bin_here < bins - 1)
+        def _():
+            rim_copy(hi, left, 0, 1).start()
+
+        @pl.when(bin_here > 0)
+        def _():
+            rim_copy(lo, right, 2, -1).start()
+
+    lax.fori_loop(bins // 2, bins, begin, 0)
+    if prepare:
+        dip_rows, nmo_weights = tables
+        matrix, weights = results
+        dip_matrix(dip_rows, matrix)
+
+        def turn(block, carry):
+            lanes = pl.ds(pl.multiple_of(128 * block, 128), 128)
+            weights[:, :, lanes] = jnp.transpose(
+                nmo_weights[:, :, lanes].astype(jnp.float32), (1, 0, 2)
+            )
+            return carry
+
+        lax.fori_loop(0, nmo_weights.shape[2] // 128, turn, 0)
+    if halo:
+
+        @pl.when(bin_here == 0)
+        def _():
+            left[...] = jnp.zeros(left.shape, left.dtype)
+
+        @pl.when(bin_here == bins - 1)
+        def _():
+            right[...] = jnp.zeros(right.shape, right.dtype)
+
     for copy in own:
         copy.wait()
-    lax.fori_loop(1, count, finish, 0)
-
-
-def exchange(arrays, collective_id):
+    lax.fori_loop(0, bins, each(lambda copy: copy.wait()), 0)
+    if halo:
+
+        @pl.when(bin_here < bins - 1)
+        def _():
+            rim_copy(hi, left, 0, 1).wait_send()
+            rim_copy(lo, right, 2, 1).wait_recv()
+
+        @pl.when(bin_here > 0)
+        def _():
+            rim_copy(lo, right, 2, -1).wait_send()
+            rim_copy(hi, left, 0, -1).wait_recv()
+
+
+def dip_matrix(dip_rows, matrix):
+    taps = dip_rows.shape[0]
+    matrix[:256, 128:] = jnp.zeros((256, 128), jnp.bfloat16)
+    matrix[256 * taps :, :128] = jnp.zeros((256, 128), jnp.bfloat16)
+    for tap in range(taps):
+        one = toeplitz(dip_rows[tap : tap + 1, :])[:, :128].astype(jnp.bfloat16)
+        matrix[256 * tap : 256 * tap + 256, :128] = one
+        matrix[256 * tap + 256 : 256 * tap + 512, 128:] = one
+
+
+def exchange(arrays, collective_id, halo=(), tables=()):
     shots, bins = lax.axis_size("shot"), lax.axis_size("bin")
     count = shots * bins
     number = len(arrays)
+    shapes = [jax.ShapeDtypeStruct(array.shape, array.dtype) for array in arrays]
+    if tables:
+        dip_rows, nmo_weights = tables
+        offsets, taps, samples = nmo_weights.shape
+        shapes.append(jax.ShapeDtypeStruct(((dip_rows.shape[0] + 1) * 256, 256), jnp.bfloat16))
+        shapes.append(jax.ShapeDtypeStruct((taps, offsets, samples), jnp.float32))
+    shapes += [jax.ShapeDtypeStruct(array.shape, array.dtype) for array in halo]
+    operands = [*arrays, *tables, *halo]
+    vmem = pl.BlockSpec(memory_space=pltpu.VMEM)
     return pl.pallas_call(
-        functools.partial(exchange_kernel, shots, bins, number),
-        out_shape=[jax.ShapeDtypeStruct(array.shape, array.dtype) for array in arrays],
-        in_specs=[pl.BlockSpec(memory_space=pltpu.VMEM)] * number,
-        out_specs=[pl.BlockSpec(memory_space=pltpu.VMEM)] * number,
+        functools.partial(exchange_kernel, shots, bins, number, bool(halo), bool(tables)),
+        out_shape=shapes,
+        in_specs=[vmem] * len(operands),
+        out_specs=[vmem] * len(shapes),
         scratch_shapes=[pltpu.SemaphoreType.DMA((count,)) for _ in range(2 * number)]
-        + [pltpu.SemaphoreType.DMA((number,))],
+        + [pltpu.SemaphoreType.DMA((number,)), pltpu.SemaphoreType.DMA((4,))],
         compiler_params=pltpu.CompilerParams(
             collective_id=collective_id, has_side_effects=True, vmem_limit_bytes=VMEM_BYTES
         ),
         name=f"exchange_{collective_id}",
-    )(*arrays)
+    )(*operands)
 
 
 def bin_kernel(capacity, cells_here, arrived, codes, lo, hi):
@@ -201,7 +278,7 @@
     inputs = refs[: 4 * len(halves)]
     rest = refs[4 * len(halves) :]
     earlier = rest[0] if first_block else None
-    dip_rows, start, weights, out, ext, matrix, ring, staged, sems = rest[1 if first_block else 0 :]
+    matrix, start, weights, out, ext, ring, staged, sems = rest[1 if first_block else 0 :]
     crosslines, offsets = ext.shape[1], ext.shape[2]
     blocks = ext.shape[3] // 128 - 2
     half = crosslines // 4
@@ -223,12 +300,6 @@
             ext[:, :, :, low:high] = jnp.zeros(
                 (IL_DEV, crosslines, offsets, high - low), jnp.bfloat16
             )
-    matrix[:256, 128:] = jnp.zeros((256, 128), jnp.bfloat16)
-    matrix[256 * taps :, :128] = jnp.zeros((256, 128), jnp.bfloat16)
-    for tap in range(taps):
-        one = toeplitz(dip_rows[tap : tap + 1, :])[:, :128].astype(jnp.bfloat16)
-        matrix[256 * tap : 256 * tap + 256, :128] = one
-        matrix[256 * tap + 256 : 256 * tap + 512, 128:] = one
     if first_block:
         out[:, :, : 128 * first_block] = earlier[...]
     for copy in copies:
@@ -315,31 +386,32 @@
     parts = 2
     span = samples // parts
     row = jax.ShapeDtypeStruct((slots, span), jnp.bfloat16)
-    line = pltpu.VMEM((1, trace_count), jnp.int32)
+    width = max(trace_count, 256)
+
+    def wide(array, before=0):
+        array = array.astype(jnp.float32).reshape(-1, array.shape[-1])
+        return jnp.pad(array, ((0, 0), (before, width - before - array.shape[1])))
+
+    table = jnp.concatenate(
+        [
+            wide(bin_owner.reshape(trace_count)),
+            wide(bin_slot),
+            wide(offset_class),
+            wide(channel_gain),
+            wide(shot_filter, 128),
+        ]
+    )
     *outgoing, codes = pl.pallas_call(
-        functools.partial(decon_kernel, owners, capacity, offsets),
+        functools.partial(decon_kernel, owners, capacity, offsets, shot_filter.shape[0]),
         out_shape=[row] * parts + [jax.ShapeDtypeStruct((owners, 1, 128), jnp.float32)],
-        in_specs=[pl.BlockSpec(memory_space=pltpu.HBM)] * 5 + [vmem],
+        in_specs=[vmem] * 2,
         out_specs=[vmem] * (parts + 1),
         scratch_shapes=[
             pltpu.VMEM(traces.shape, jnp.bfloat16),
-            pltpu.VMEM((1, channel_gain.shape[0]), jnp.float32),
-            line,
-            line,
-            line,
-            pltpu.VMEM(traces.shape, jnp.bfloat16),
-            pltpu.SemaphoreType.DMA((5,)),
         ],
         compiler_params=params,
         name="decon",
-    )(
-        traces,
-        channel_gain[None, :],
-        bin_owner.reshape(1, trace_count),
-        bin_slot[None, :],
-        offset_class[None, :],
-        shot_filter,
-    )
+    )(traces, table)
 
     taps, time_taps = dip_filter.shape
     before = 192 + time_taps // 2 - (time_taps - 1)
@@ -347,7 +419,6 @@
         dip_filter[:, ::-1].astype(jnp.float32),
         ((0, 0), (before, 256 - before - time_taps)),
     )
-    weights = jnp.transpose(nmo_weights, (1, 0, 2)).astype(jnp.float32)
     crosslines = 2 * XL_DEV
 
     rim = jax.ShapeDtypeStruct((IL_DEV, half, offsets, span), jnp.bfloat16)
@@ -355,9 +426,12 @@
     for part in range(parts):
         rows = outgoing[part].reshape(owners, capacity, span)
         if part == 0:
-            arrived, codes = exchange([rows, codes], 1)
+            arrived, codes, matrix, weights = exchange(
+                [rows, codes], 1, tables=(dip_rows, nmo_weights)
+            )
         else:
-            (arrived,) = exchange([rows], 1 + part)
+            arrived, left, right = exchange([rows], 1 + part, halo=(lo, hi))
+            sides.append((left, lo, hi, right))
         lo, hi = pl.pallas_call(
             functools.partial(bin_kernel, capacity, cells_here),
             out_shape=(rim, rim),
@@ -366,9 +440,9 @@
             compiler_params=params,
             name=f"bin_{part}",
         )(arrived.reshape(slots, span), codes)
-        right = lax.ppermute(lo, "bin", [(i + 1, i) for i in range(bins - 1)])
-        left = lax.ppermute(hi, "bin", [(i, i + 1) for i in range(bins - 1)])
-        sides.append((left, lo, hi, right))
+    right = lax.ppermute(lo, "bin", [(i + 1, i) for i in range(bins - 1)])
+    left = lax.ppermute(hi, "bin", [(i, i + 1) for i in range(bins - 1)])
+    sides.append((left, lo, hi, right))
 
     per_part = span // 128
     total = samples // 128
@@ -394,14 +468,13 @@
             out_specs=vmem,
             scratch_shapes=[
                 pltpu.VMEM((IL_DEV, crosslines, offsets, 128 * (blocks + 2)), jnp.bfloat16),
-                pltpu.VMEM(((taps + 1) * 256, 256), jnp.bfloat16),
                 pltpu.VMEM((3, IL_DEV, XL_DEV // 2, 2, offsets, 128), jnp.float32),
                 pltpu.VMEM((IL_DEV, XL_DEV // 2, 2, offsets, 128), jnp.float32),
                 pltpu.SemaphoreType.DMA((4 * len(halves),)),
             ],
             compiler_params=params,
             name=f"stack_{part}",
-        )(*operands, *([stacked] if first else []), dip_rows, nmo_start, weights)
+        )(*operands, *([stacked] if first else []), matrix, nmo_start, weights)
     return stacked
 
 

time: 108 us -> 101 us (0.935)
  starting transfers between devices: 12.8 us -> 4.33 us
    ppermute x2 -> x1, starting transfers between devices: 8.97 us -> 2.29 us  [per_device(): left = lax.ppermute(hi, 'bin', [(i, i + 1) for i in range(bins - 1)])]
    unnamed x16 -> x6, local copies, waits for them, and re-layouts: 4.61 us -> 2.44 us
    ppermute x2 -> x1, starting transfers between devices: 3.84 us -> 2.04 us  [per_device(): right = lax.ppermute(lo, 'bin', [(i + 1, i) for i in range(bins - 1)])]
    pallas_call x3, Pallas kernels: 58.8 us -> 59.9 us  [the longest x2 58.5 us: exchange(): pl.pallas_call(functools.partial(exchange_kernel, shots, bins, number, bo...]
  transfers between devices with their start and end apart: 4 -> 2, of which waited for: 1 -> 1; matrix products, arithmetic and copies ran while one was open for 2% -> 0% of each run, Pallas kernels for 38% -> 10%
where the time goes in v4:
time: 101 us; the launch traced here: 99.3 us
  Pallas kernels  87 us (86%)
  starting transfers between devices  4.33 us (4%)
  local copies, waits for them, and re-layouts  3.91 us (4%)
  other arithmetic  2.78 us (3%)
  waiting for transfers between devices  1.17 us (1%)
    pallas_call x2, Pallas kernels, exchange(): pl.pallas_call(functools.partial(exchange_kernel, shots, bins, number, bo...  58.5 us
    pallas_call x2, Pallas kernels, per_device(): pl.pallas_call(functools.partial(stack_kernel, taps, first, halves), out_...  24.2 us
    pallas_call x2, Pallas kernels, per_device(): pl.pallas_call(functools.partial(bin_kernel, capacity, cells_here), out_s...  2.9 us
    unnamed x6, local copies, waits for them, and re-layouts  2.44 us
    ppermute x1, starting transfers between devices, per_device(): left = lax.ppermute(hi, 'bin', [(i, i + 1) for i in range(bins - 1)])  2.29 us
    convert_element_type x3, other arithmetic, wide(): array = array.astype(jnp.float32).reshape(-1, array.shape[-1])  2.04 us
    ppermute x1, starting transfers between devices, per_device(): right = lax.ppermute(lo, 'bin', [(i + 1, i) for i in range(bins - 1)])  2.04 us
  transfers between devices with their start and end apart: 2, of which 1 were waited for; matrix products, arithmetic and copies ran while one was open for 0% of the time, Pallas kernels for 10%

profile of v4, /device:TPU:11, one launch (start us, length us, event | category | flops | bytes accessed | tf_op | source)
XLA Modules:
  0.0 99.3 jit_solution(5952749480043235339)
XLA Ops:
  0.0 0.7 pad_convert_fusion.1
  0.7 0.7 convert_bitcast_fusion
  1.3 0.7 convert_element_type.27
  2.0 0.7 convert_element_type.28
  2.7 0.8 rev.3
  3.5 0.1 pad_convert_fusion.refs_2_
  3.5 0.7 concatenate.3.table
  4.2 0.0 copy-start.1
  4.3 1.2 %copy-done.1 = bf16[256,2048]{1,0:T(8,128)(2,1)S(1)} copy-done((bf16[256,2048]{1,0:T(8,128)(2,1)S(1)}, bf16[256,2048]{1,0:T(8,128)(2,1)}, u32[]{:S(2)}) %copy-start.1) | copy-done | bytes 1048600
  5.5 1.5 %decon.1 = (bf16[512,1024]{1,0:T(8,128)(2,1)S(1)}, bf16[512,1024]{1,0:T(8,128)(2,1)S(1)}, f32[32,1,128]{2,1,0:T(1,128)S(1)}) custom-call(bf16[256,2048]{1,0:T(8,128)(2,1)S(1)} %copy-done.1, f32[5,256]{1,0:T(8,128)S(1)} %concatenate.3.table), custom_call_target="tpu_custom_call" | custom-call | tf_op jit(solution)/shard_map/decon/pallas_call | solution.py:404
  6.9 0.0 copy-start.2
  6.9 1.2 %copy-done.2 = bf16[32,8,2048]{2,1,0:T(8,128)(2,1)S(1)} copy-done((bf16[32,8,2048]{2,1,0:T(8,128)(2,1)S(1)}, bf16[32,8,2048]{2,1,0:T(8,128)(2,1)}, u32[]{:S(2)}) %copy-start.2) | copy-done | bytes 1048600
  8.2 30.2 %exchange_1.1 = (bf16[32,16,1024]{2,1,0:T(8,128)(2,1)S(1)}, f32[32,1,128]{2,1,0:T(1,128)S(1)}, bf16[2560,256]{1,0:T(8,128)(2,1)S(1)}, f32[8,32,2048]{2,1,0:T(8,128)S(1)}) custom-call(bf16[32,16,1024]{2,1,0:T(8,128)(2,1)S(1)} %bitcast.10, f32[32,1,128]{2,1,0:T(1,128)S(1)} %get-tuple-element.21.refs_1_, f32[9,256]{1,0:T(8,128)S(1)} %pad_convert_fusion.refs_2_, ...), custom_call_target="tpu_custom_call" | custom-call | tf_op jit(solution)/shard_map/exchange_1/pallas_call | solution.py:239
  38.4 0.0 copy-start
  38.4 1.5 %bin_0.1 = (bf16[2,4,32,1024]{3,2,1,0:T(8,128)(2,1)S(1)}, bf16[2,4,32,1024]{3,2,1,0:T(8,128)(2,1)S(1)}) custom-call(bf16[512,1024]{1,0:T(8,128)(2,1)S(1)} %bitcast.11, f32[32,1,128]{2,1,0:T(1,128)S(1)} %get-tuple-element.23.codes), custom_call_target="tpu_custom_call" | custom-call | tf_op jit(solution)/shard_map/bin_0/pallas_call | solution.py:435
  39.9 28.2 %exchange_2.1 = (bf16[32,16,1024]{2,1,0:T(8,128)(2,1)S(1)}, bf16[2,4,32,1024]{3,2,1,0:T(8,128)(2,1)S(1)}, bf16[2,4,32,1024]{3,2,1,0:T(8,128)(2,1)S(1)}) custom-call(bf16[32,16,1024]{2,1,0:T(8,128)(2,1)S(1)} %bitcast.9, bf16[2,4,32,1024]{3,2,1,0:T(8,128)(2,1)S(1)} %get-tuple-element.24.refs_1_, bf16[2,4,32,1024]{3,2,1,0:T(8,128)(2,1)S(1)} %get-tuple-element.25.refs_2_), custom_call_target="tpu_custom_call" | custom-call | tf_op jit(solution)/shard_map/exchange_2/pallas_call | solution.py:239
  68.1 1.5 %bin_1.1 = (bf16[2,4,32,1024]{3,2,1,0:T(8,128)(2,1)S(1)}, bf16[2,4,32,1024]{3,2,1,0:T(8,128)(2,1)S(1)}) custom-call(bf16[512,1024]{1,0:T(8,128)(2,1)S(1)} %bitcast.12, f32[32,1,128]{2,1,0:T(1,128)S(1)} %get-tuple-element.23.codes), custom_call_target="tpu_custom_call" | custom-call | tf_op jit(solution)/shard_map/bin_1/pallas_call | solution.py:435
  69.6 2.3 %collective-permute-start = (bf16[2,4,32,1024]{3,2,1,0:T(8,128)(2,1)S(1)}, bf16[2,4,32,1024]{3,2,1,0:T(8,128)(2,1)S(1)}, u32[]{:S(2)}, u32[]{:S(2)}) collective-permute-start(bf16[2,4,32,1024]{3,2,1,0:T(8,128)(2,1)S(1)} %get-tuple-element.29.refs_6_), channel_id=1, source_target_pairs={{0,1},{1,2},{2,3},{3,4},{4,5},{5,6},{6,7},{8,9},{9,10},{10,11},{11... | collective-permute-start | bytes 1572872 | tf_op jit(solution)/shard_map/ppermute | solution.py:444
  71.9 2.0 %collective-permute-start.1 = (bf16[2,4,32,1024]{3,2,1,0:T(8,128)(2,1)S(1)}, bf16[2,4,32,1024]{3,2,1,0:T(8,128)(2,1)S(1)}, u32[]{:S(2)}, u32[]{:S(2)}) collective-permute-start(bf16[2,4,32,1024]{3,2,1,0:T(8,128)(2,1)S(1)} %get-tuple-element.30.refs_5_), channel_id=1, source_target_pairs={{1,0},{2,1},{3,2},{4,3},{5,4},{6,5},{7,6},{9,8},{10,9},{11,10},{12... | collective-permute-start | bytes 1572872 | tf_op jit(solution)/shard_map/ppermute | solution.py:443
  73.9 0.0 copy-done
  73.9 10.4 %stack_0.1.refs_8_ = f32[2,8,896]{2,1,0:T(8,128)S(1)} custom-call(bf16[2,4,32,1024]{3,2,1,0:T(8,128)(2,1)S(1)} %get-tuple-element.26.refs_0_, bf16[2,4,32,1024]{3,2,1,0:T(8,128)(2,1)S(1)} %get-tuple-element.24.refs_1_, bf16[2,4,32,1024]{3,2,1,0:T(8,128)(2,1)S(1)} %get-tuple-element.25.refs_2_, bf16[2,4,32,1024]{3,2,1,0:T(8,128)(2,1)S(1)} %get-tuple-element.27.refs_3_, ...), custom_call_target="tpu_custom_call" | custom-call | tf_op jit(solution)/shard_map/stack_0/pallas_call | solution.py:464
  84.3 0.0 collective-permute-done.refs_4_
  84.3 1.2 %collective-permute-done.1.refs_7_ = bf16[2,4,32,1024]{3,2,1,0:T(8,128)(2,1)S(1)} collective-permute-done((bf16[2,4,32,1024]{3,2,1,0:T(8,128)(2,1)S(1)}, bf16[2,4,32,1024]{3,2,1,0:T(8,128)(2,1)S(1)}, u32[]{:S(2)}, u32[]{:S(2)}) %collective-permute-start.1) | collective-permute-done | bytes 524320 | tf_op jit(solution)/shard_map/ppermute | solution.py:443
  85.5 13.8 %stack_1.1 = f32[2,8,2048]{2,1,0:T(8,128)} custom-call(bf16[2,4,32,1024]{3,2,1,0:T(8,128)(2,1)S(1)} %get-tuple-element.26.refs_0_, bf16[2,4,32,1024]{3,2,1,0:T(8,128)(2,1)S(1)} %get-tuple-element.24.refs_1_, bf16[2,4,32,1024]{3,2,1,0:T(8,128)(2,1)S(1)} %get-tuple-element.25.refs_2_, bf16[2,4,32,1024]{3,2,1,0:T(8,128)(2,1)S(1)} %get-tuple-element.27.refs_3_, ...), custom_call_target="tpu_custom_call" | custom-call | tf_op jit(solution)/shard_map/stack_1/pallas_call | solution.py:464
Async XLA Ops:
  4.2 1.2 %copy-start.1 = (bf16[256,2048]{1,0:T(8,128)(2,1)S(1)}, bf16[256,2048]{1,0:T(8,128)(2,1)}, u32[]{:S(2)}) copy-start(bf16[256,2048]{1,0:T(8,128)(2,1)} %traces.1) | copy-start | bytes 3145732
  6.9 1.2 %copy-start.2 = (bf16[32,8,2048]{2,1,0:T(8,128)(2,1)S(1)}, bf16[32,8,2048]{2,1,0:T(8,128)(2,1)}, u32[]{:S(2)}) copy-start(bf16[32,8,2048]{2,1,0:T(8,128)(2,1)} %refs_3_.1) | copy-start | bytes 3145732
  38.4 35.5 %copy-start = (s32[32,2048]{1,0:T(8,128)S(1)}, s32[32,2048]{1,0:T(8,128)}, u32[]{:S(2)}) copy-start(s32[32,2048]{1,0:T(8,128)} %refs_10_.1) | copy-start | bytes 786436
  69.6 14.8 %collective-permute-start = (bf16[2,4,32,1024]{3,2,1,0:T(8,128)(2,1)S(1)}, bf16[2,4,32,1024]{3,2,1,0:T(8,128)(2,1)S(1)}, u32[]{:S(2)}, u32[]{:S(2)}) collective-permute-start(bf16[2,4,32,1024]{3,2,1,0:T(8,128)(2,1)S(1)} %get-tuple-element.29.refs_6_), channel_id=1, source_target_pairs={{0,1},{1,2},{2,3},{3,4},{4,5},{5,6},{6,7},{8,9},{9,10},{10,11},{11... | collective-permute-start | bytes 1572872 | tf_op jit(solution)/shard_map/ppermute | solution.py:444
  71.9 13.6 %collective-permute-start.1 = (bf16[2,4,32,1024]{3,2,1,0:T(8,128)(2,1)S(1)}, bf16[2,4,32,1024]{3,2,1,0:T(8,128)(2,1)S(1)}, u32[]{:S(2)}, u32[]{:S(2)}) collective-permute-start(bf16[2,4,32,1024]{3,2,1,0:T(8,128)(2,1)S(1)} %get-tuple-element.30.refs_5_), channel_id=1, source_target_pairs={{1,0},{2,1},{3,2},{4,3},{5,4},{6,5},{7,6},{9,8},{10,9},{11,10},{12... | collective-permute-start | bytes 1572872 | tf_op jit(solution)/shard_map/ppermute | solution.py:443

commit v5 on v4

--- a/solution.py
+++ b/solution.py
@@ -81,23 +81,29 @@
             ).astype(jnp.bfloat16)
 
 
-def exchange_kernel(shots, bins, arrays, halo, prepare, *refs):
+def exchange_kernel(
+    shots,
+    bins,
+    capacity,
+    cells_here,
+    rows_0,
+    names,
+    rows_1,
+    nmo_weights,
+    names_in,
+    arrived_1,
+    weights,
+    lo,
+    hi,
+    left,
+    right,
+    arrived_0,
+    send_sems,
+    recv_sems,
+    own_sem,
+    halo_sem,
+):
     count = shots * bins
-    refs = list(refs)
-
-    def take(number):
-        taken = refs[:number]
-        del refs[:number]
-        return taken
-
-    sources = take(arrays)
-    tables = take(2) if prepare else None
-    lo, hi = take(2) if halo else (None, None)
-    targets = take(arrays)
-    results = take(2) if prepare else None
-    left, right = take(2) if halo else (None, None)
-    send_sems, recv_sems = take(arrays), take(arrays)
-    own_sem, halo_sem = refs
     here, bin_here = lax.axis_index("shot"), lax.axis_index("bin")
     me = here * bins + bin_here
     barrier = pltpu.get_barrier_semaphore()
@@ -110,46 +116,45 @@
         return carry
 
     lax.fori_loop(1, count, greet, 0)
+    moved = ((names, names_in), (rows_0, arrived_0), (rows_1, arrived_1))
     own = [
-        pltpu.make_async_copy(sources[k].at[me], targets[k].at[me], own_sem.at[k])
-        for k in range(arrays)
+        pltpu.make_async_copy(source.at[me], target.at[me], own_sem.at[k])
+        for k, (source, target) in enumerate(moved)
     ]
     for copy in own:
         copy.start()
     pl.semaphore_wait(barrier, count - 1)
 
-    def copies_of(shot_step, bin_step):
+    def copy_of(k, shot_step, bin_step):
+        source, target = moved[k]
         shot = lax.rem(here + shot_step, shots)
         crossline = lax.rem(bin_here + bin_step, bins)
-        other = shot * bins + crossline
-        return [
-            pltpu.make_async_remote_copy(
-                src_ref=sources[k].at[other],
-                dst_ref=targets[k].at[me],
-                send_sem=send_sems[k].at[shot_step * bins + bin_step],
-                recv_sem=recv_sems[k].at[shot_step * bins + bin_step],
-                device_id=(shot, crossline),
-                device_id_type=MESH,
-            )
-            for k in range(arrays)
-        ]
+        step = shot_step * bins + bin_step
+        return pltpu.make_async_remote_copy(
+            src_ref=source.at[shot * bins + crossline],
+            dst_ref=target.at[me],
+            send_sem=send_sems.at[k, step],
+            recv_sem=recv_sems.at[k, step],
+            device_id=(shot, crossline),
+            device_id_type=MESH,
+        )
 
     far_first = sorted(range(1, shots), key=lambda step: -min(step, shots - step))
 
-    def each(action):
+    def each(parts, action):
         def one(bin_step, carry):
             for shot_step in far_first:
-                for copy in copies_of(shot_step, bin_step):
-                    action(copy)
+                for k in parts:
+                    action(copy_of(k, shot_step, bin_step))
 
             @pl.when(bin_step > 0)
             def _():
-                for copy in copies_of(0, bin_step):
-                    action(copy)
+                for k in parts:
+                    action(copy_of(k, 0, bin_step))
 
             return carry
 
-        return one
+        lax.fori_loop(0, bins, one, 0)
 
     def rim_copy(source, target, sem, step):
         return pltpu.make_async_remote_copy(
@@ -161,99 +166,57 @@
             device_id_type=MESH,
         )
 
-    begin = each(lambda copy: copy.start())
-    lax.fori_loop(0, bins // 2, begin, 0)
-    if halo:
-
-        @pl.when(bin_here < bins - 1)
-        def _():
-            rim_copy(hi, left, 0, 1).start()
-
-        @pl.when(bin_here > 0)
-        def _():
-            rim_copy(lo, right, 2, -1).start()
-
-    lax.fori_loop(bins // 2, bins, begin, 0)
-    if prepare:
-        dip_rows, nmo_weights = tables
-        matrix, weights = results
-        dip_matrix(dip_rows, matrix)
-
-        def turn(block, carry):
-            lanes = pl.ds(pl.multiple_of(128 * block, 128), 128)
-            weights[:, :, lanes] = jnp.transpose(
-                nmo_weights[:, :, lanes].astype(jnp.float32), (1, 0, 2)
-            )
-            return carry
-
-        lax.fori_loop(0, nmo_weights.shape[2] // 128, turn, 0)
-    if halo:
-
-        @pl.when(bin_here == 0)
-        def _():
-            left[...] = jnp.zeros(left.shape, left.dtype)
-
-        @pl.when(bin_here == bins - 1)
-        def _():
-            right[...] = jnp.zeros(right.shape, right.dtype)
-
-    for copy in own:
-        copy.wait()
-    lax.fori_loop(0, bins, each(lambda copy: copy.wait()), 0)
-    if halo:
-
-        @pl.when(bin_here < bins - 1)
-        def _():
-            rim_copy(hi, left, 0, 1).wait_send()
-            rim_copy(lo, right, 2, 1).wait_recv()
-
-        @pl.when(bin_here > 0)
-        def _():
-            rim_copy(lo, right, 2, -1).wait_send()
-            rim_copy(hi, left, 0, -1).wait_recv()
-
-
-def dip_matrix(dip_rows, matrix):
-    taps = dip_rows.shape[0]
-    matrix[:256, 128:] = jnp.zeros((256, 128), jnp.bfloat16)
-    matrix[256 * taps :, :128] = jnp.zeros((256, 128), jnp.bfloat16)
-    for tap in range(taps):
-        one = toeplitz(dip_rows[tap : tap + 1, :])[:, :128].astype(jnp.bfloat16)
-        matrix[256 * tap : 256 * tap + 256, :128] = one
-        matrix[256 * tap + 256 : 256 * tap + 512, 128:] = one
-
-
-def exchange(arrays, collective_id, halo=(), tables=()):
-    shots, bins = lax.axis_size("shot"), lax.axis_size("bin")
-    count = shots * bins
-    number = len(arrays)
-    shapes = [jax.ShapeDtypeStruct(array.shape, array.dtype) for array in arrays]
-    if tables:
-        dip_rows, nmo_weights = tables
-        offsets, taps, samples = nmo_weights.shape
-        shapes.append(jax.ShapeDtypeStruct(((dip_rows.shape[0] + 1) * 256, 256), jnp.bfloat16))
-        shapes.append(jax.ShapeDtypeStruct((taps, offsets, samples), jnp.float32))
-    shapes += [jax.ShapeDtypeStruct(array.shape, array.dtype) for array in halo]
-    operands = [*arrays, *tables, *halo]
-    vmem = pl.BlockSpec(memory_space=pltpu.VMEM)
-    return pl.pallas_call(
-        functools.partial(exchange_kernel, shots, bins, number, bool(halo), bool(tables)),
-        out_shape=shapes,
-        in_specs=[vmem] * len(operands),
-        out_specs=[vmem] * len(shapes),
-        scratch_shapes=[pltpu.SemaphoreType.DMA((count,)) for _ in range(2 * number)]
-        + [pltpu.SemaphoreType.DMA((number,)), pltpu.SemaphoreType.DMA((4,))],
-        compiler_params=pltpu.CompilerParams(
-            collective_id=collective_id, has_side_effects=True, vmem_limit_bytes=VMEM_BYTES
-        ),
-        name=f"exchange_{collective_id}",
-    )(*operands)
-
-
-def bin_kernel(capacity, cells_here, arrived, codes, lo, hi):
-    owners = codes.shape[0]
-    slots, samples = arrived.shape
-    listed = codes[:, 0, :]
+    each((0, 1), lambda copy: copy.start())
+    each((2,), lambda copy: copy.start())
+
+    def turn(block, carry):
+        lanes = pl.ds(pl.multiple_of(128 * block, 128), 128)
+        weights[:, :, lanes] = jnp.transpose(
+            nmo_weights[:, :, lanes].astype(jnp.float32), (1, 0, 2)
+        )
+        return carry
+
+    lax.fori_loop(0, nmo_weights.shape[2] // 128, turn, 0)
+
+    @pl.when(bin_here == 0)
+    def _():
+        left[...] = jnp.zeros(left.shape, left.dtype)
+
+    @pl.when(bin_here == bins - 1)
+    def _():
+        right[...] = jnp.zeros(right.shape, right.dtype)
+
+    own[0].wait()
+    own[1].wait()
+    each((0, 1), lambda copy: copy.wait())
+    bin_rows(capacity, cells_here, arrived_0, names_in, lo, hi)
+
+    @pl.when(bin_here < bins - 1)
+    def _():
+        rim_copy(hi, left, 0, 1).start()
+
+    @pl.when(bin_here > 0)
+    def _():
+        rim_copy(lo, right, 2, -1).start()
+
+    own[2].wait()
+    each((2,), lambda copy: copy.wait())
+
+    @pl.when(bin_here < bins - 1)
+    def _():
+        rim_copy(hi, left, 0, 1).wait_send()
+        rim_copy(lo, right, 2, 1).wait_recv()
+
+    @pl.when(bin_here > 0)
+    def _():
+        rim_copy(lo, right, 2, -1).wait_send()
+        rim_copy(hi, left, 0, -1).wait_recv()
+
+
+def bin_rows(capacity, cells_here, arrived, names, lo, hi):
+    owners, slots_each, samples = arrived.shape
+    slots = owners * slots_each
+    listed = names[:, 0, :]
     place = iota((owners, slots), 1) - capacity * iota((owners, slots), 0)
     spread = jnp.zeros((owners, slots), jnp.float32)
     for rank in range(capacity):
@@ -265,20 +228,71 @@
     member = member_f.astype(jnp.bfloat16)
     offsets = lo.shape[2]
     half = XL_DEV // 2
-    for lane in range(0, samples, 256):
-        summed = jnp.dot(
-            member, arrived[:, lane : lane + 256], preferred_element_type=jnp.float32
-        )
+
+    def chunk(number, carry):
+        lanes = pl.ds(pl.multiple_of(256 * number, 256), 256)
+        rows = arrived[:, :, lanes]
+        if capacity % 16:
+            rows = rows.astype(jnp.float32).reshape(slots, 256).astype(jnp.bfloat16)
+        summed = jnp.dot(member, rows.reshape(slots, 256), preferred_element_type=jnp.float32)
         binned = (summed * scale).astype(jnp.bfloat16).reshape(IL_DEV, XL_DEV, offsets, 256)
-        lo[:, :, :, lane : lane + 256] = binned[:, :half]
-        hi[:, :, :, lane : lane + 256] = binned[:, half:]
-
-
-def stack_kernel(taps, first_block, halves, *refs):
+        lo[:, :, :, lanes] = binned[:, :half]
+        hi[:, :, :, lanes] = binned[:, half:]
+        return carry
+
+    lax.fori_loop(0, samples // 256, chunk, 0)
+
+
+def dip_matrix(dip_rows, matrix):
+    taps = dip_rows.shape[0]
+    matrix[:256, 128:] = jnp.zeros((256, 128), jnp.bfloat16)
+    matrix[256 * taps :, :128] = jnp.zeros((256, 128), jnp.bfloat16)
+    for tap in range(taps):
+        one = toeplitz(dip_rows[tap : tap + 1, :])[:128].T.astype(jnp.bfloat16)
+        matrix[256 * tap : 256 * tap + 256, :128] = one
+        matrix[256 * tap + 256 : 256 * tap + 512, 128:] = one
+
+
+def exchange(rows_0, names, rows_1, nmo_weights, cells_here, rim):
+    shots, bins = lax.axis_size("shot"), lax.axis_size("bin")
+    count = shots * bins
+    offsets, taps, samples = nmo_weights.shape
+
+    def like(array):
+        return jax.ShapeDtypeStruct(array.shape, array.dtype)
+
+    vmem = pl.BlockSpec(memory_space=pltpu.VMEM)
+    return pl.pallas_call(
+        functools.partial(exchange_kernel, shots, bins, rows_0.shape[1], cells_here),
+        out_shape=[
+            like(names),
+            like(rows_1),
+            jax.ShapeDtypeStruct((taps, offsets, samples), jnp.float32),
+        ]
+        + [rim] * 4,
+        in_specs=[vmem] * 4,
+        out_specs=[vmem] * 7,
+        scratch_shapes=[
+            pltpu.VMEM(rows_0.shape, rows_0.dtype),
+            pltpu.SemaphoreType.DMA((3, count)),
+            pltpu.SemaphoreType.DMA((3, count)),
+            pltpu.SemaphoreType.DMA((3,)),
+            pltpu.SemaphoreType.DMA((4,)),
+        ],
+        compiler_params=pltpu.CompilerParams(
+            collective_id=1, has_side_effects=True, vmem_limit_bytes=VMEM_BYTES
+        ),
+        name="exchange",
+    )(rows_0, names, rows_1, nmo_weights)
+
+
+def stack_kernel(taps, first_block, dip_row, halves, *refs):
     inputs = refs[: 4 * len(halves)]
     rest = refs[4 * len(halves) :]
-    earlier = rest[0] if first_block else None
-    matrix, start, weights, out, ext, ring, staged, sems = rest[1 if first_block else 0 :]
+    if first_block:
+        earlier, matrix, start, weights, out, ext, ring, staged, sems = rest
+    else:
+        table, start, weights, out, matrix, ext, ring, staged, sems = rest
     crosslines, offsets = ext.shape[1], ext.shape[2]
     blocks = ext.shape[3] // 128 - 2
     half = crosslines // 4
@@ -300,7 +314,9 @@
             ext[:, :, :, low:high] = jnp.zeros(
                 (IL_DEV, crosslines, offsets, high - low), jnp.bfloat16
             )
-    if first_block:
+    if not first_block:
+        dip_matrix(table[dip_row : dip_row + taps, :256], matrix)
+    else:
         out[:, :, : 128 * first_block] = earlier[...]
     for copy in copies:
         copy.wait()
@@ -388,18 +404,29 @@
     row = jax.ShapeDtypeStruct((slots, span), jnp.bfloat16)
     width = max(trace_count, 256)
 
-    def wide(array, before=0):
-        array = array.astype(jnp.float32).reshape(-1, array.shape[-1])
-        return jnp.pad(array, ((0, 0), (before, width - before - array.shape[1])))
-
-    table = jnp.concatenate(
-        [
-            wide(bin_owner.reshape(trace_count)),
-            wide(bin_slot),
-            wide(offset_class),
-            wide(channel_gain),
-            wide(shot_filter, 128),
-        ]
+    taps, time_taps = dip_filter.shape
+    shots_here = shot_filter.shape[0]
+    dip_row = 4 + shots_here
+    height = dip_row + taps
+    lines = iota((height, width), 0)
+
+    def one_row(array, row):
+        array = array.reshape(1, -1)
+        array = jnp.pad(array, ((0, 0), (0, width - array.shape[1])))
+        return jnp.where(lines == row, array, jnp.zeros((), array.dtype))
+
+    def some_rows(array, row, before):
+        below = height - row - array.shape[0]
+        after = width - before - array.shape[1]
+        return jnp.pad(array.astype(jnp.float32), ((row, below), (before, after)))
+
+    table = (
+        (one_row(bin_owner, 0) + one_row(bin_slot, 1) + one_row(offset_class, 2)).astype(
+            jnp.float32
+        )
+        + one_row(channel_gain, 3)
+        + some_rows(shot_filter, 4, 128)
+        + some_rows(dip_filter, dip_row, 64 - time_taps // 2)
     )
     *outgoing, codes = pl.pallas_call(
         functools.partial(decon_kernel, owners, capacity, offsets, shot_filter.shape[0]),
@@ -413,33 +440,21 @@
         name="decon",
     )(traces, table)
 
-    taps, time_taps = dip_filter.shape
-    before = 192 + time_taps // 2 - (time_taps - 1)
-    dip_rows = jnp.pad(
-        dip_filter[:, ::-1].astype(jnp.float32),
-        ((0, 0), (before, 256 - before - time_taps)),
-    )
     crosslines = 2 * XL_DEV
-
     rim = jax.ShapeDtypeStruct((IL_DEV, half, offsets, span), jnp.bfloat16)
-    sides = []
-    for part in range(parts):
-        rows = outgoing[part].reshape(owners, capacity, span)
-        if part == 0:
-            arrived, codes, matrix, weights = exchange(
-                [rows, codes], 1, tables=(dip_rows, nmo_weights)
-            )
-        else:
-            arrived, left, right = exchange([rows], 1 + part, halo=(lo, hi))
-            sides.append((left, lo, hi, right))
-        lo, hi = pl.pallas_call(
-            functools.partial(bin_kernel, capacity, cells_here),
-            out_shape=(rim, rim),
-            in_specs=[vmem] * 2,
-            out_specs=(vmem, vmem),
-            compiler_params=params,
-            name=f"bin_{part}",
-        )(arrived.reshape(slots, span), codes)
+    rows_0, rows_1 = (rows.reshape(owners, capacity, span) for rows in outgoing)
+    codes, arrived, weights, lo, hi, left, right = exchange(
+        rows_0, codes, rows_1, nmo_weights, cells_here, rim
+    )
+    sides = [(left, lo, hi, right)]
+    lo, hi = pl.pallas_call(
+        functools.partial(bin_rows, capacity, cells_here),
+        out_shape=(rim, rim),
+        in_specs=[vmem] * 2,
+        out_specs=(vmem, vmem),
+        compiler_params=params,
+        name="bin",
+    )(arrived, codes)
     right = lax.ppermute(lo, "bin", [(i + 1, i) for i in range(bins - 1)])
     left = lax.ppermute(hi, "bin", [(i, i + 1) for i in range(bins - 1)])
     sides.append((left, lo, hi, right))
@@ -461,11 +476,14 @@
                 halves.append(
                     (128 * (begin - per_part * piece), 128 * (begin - low), 128 * (end - begin))
                 )
-        stacked = pl.pallas_call(
-            functools.partial(stack_kernel, taps, first, halves),
-            out_shape=jax.ShapeDtypeStruct((IL_DEV, XL_DEV, 128 * last), jnp.float32),
-            in_specs=[anywhere] * len(operands) + [vmem] * (4 if first else 3),
-            out_specs=vmem,
+        result = jax.ShapeDtypeStruct((IL_DEV, XL_DEV, 128 * last), jnp.float32)
+        bands = jax.ShapeDtypeStruct(((taps + 1) * 256, 256), jnp.bfloat16)
+        extra = (stacked, matrix) if first else (table,)
+        made = pl.pallas_call(
+            functools.partial(stack_kernel, taps, first, dip_row, halves),
+            out_shape=[result] if first else [result, bands],
+            in_specs=[anywhere] * len(operands) + [vmem] * (len(extra) + 2),
+            out_specs=[vmem] * (1 if first else 2),
             scratch_shapes=[
                 pltpu.VMEM((IL_DEV, crosslines, offsets, 128 * (blocks + 2)), jnp.bfloat16),
                 pltpu.VMEM((3, IL_DEV, XL_DEV // 2, 2, offsets, 128), jnp.float32),
@@ -474,7 +492,10 @@
             ],
             compiler_params=params,
             name=f"stack_{part}",
-        )(*operands, *([stacked] if first else []), matrix, nmo_start, weights)
+        )(*operands, *extra, nmo_start, weights)
+        stacked = made[0]
+        if not first:
+            matrix = made[1]
     return stacked
 
 

time: 101 us -> 97.5 us (0.965)
  other arithmetic: 2.78 us -> 0.85 us
  starting transfers between devices: 4.33 us -> 5.92 us
  local copies, waits for them, and re-layouts: 3.91 us -> 2.44 us
  waiting for transfers between devices: 1.17 us -> 0.01 us
    convert_element_type x3 -> x0, other arithmetic: 2.04 us -> none  [wide(): array = array.astype(jnp.float32).reshape(-1, array.shape[-1])]
    ppermute x1, starting transfers between devices: 2.29 us -> 4 us  [per_device(): left = lax.ppermute(hi, 'bin', [(i, i + 1) for i in range(bins - 1)])]
    ppermute x1, waiting for transfers between devices: 1.17 us -> 0.01 us  [per_device(): right = lax.ppermute(lo, 'bin', [(i + 1, i) for i in range(bins - 1)])]
    pallas_call x6 -> x4, Pallas kernels: 85.6 us -> 85.6 us  [the longest x1 58.9 us: exchange(): pl.pallas_call(functools.partial(exchange_kernel, shots, bins, rows_0.sha...]
  transfers between devices with their start and end apart: 2 -> 2, of which waited for: 1 -> 0; matrix products, arithmetic and copies ran while one was open for 0% -> 0% of each run, Pallas kernels for 10% -> 11%
where the time goes in v5:
time: 97.5 us; the launch traced here: 96.4 us
  Pallas kernels  87.1 us (89%)
  starting transfers between devices  5.92 us (6%)
  local copies, waits for them, and re-layouts  2.44 us (3%)
    pallas_call x1, Pallas kernels, exchange(): pl.pallas_call(functools.partial(exchange_kernel, shots, bins, rows_0.sha...  58.9 us
    pallas_call x2, Pallas kernels, per_device(): pl.pallas_call(functools.partial(stack_kernel, taps, first, dip_row, halv...  24.7 us
    ppermute x1, starting transfers between devices, per_device(): left = lax.ppermute(hi, 'bin', [(i, i + 1) for i in range(bins - 1)])  4 us
    unnamed x6, local copies, waits for them, and re-layouts  2.44 us
    pallas_call x1, Pallas kernels, per_device(): pl.pallas_call(functools.partial(bin_rows, capacity, cells_here), out_sha...  2.1 us
  transfers between devices with their start and end apart: 2, of which 0 were waited for; matrix products, arithmetic and copies ran while one was open for 0% of the time, Pallas kernels for 11%

profile of v5, /device:TPU:11, one launch (start us, length us, event | category | flops | bytes accessed | tf_op | source)
XLA Modules:
  0.0 96.4 jit_solution(17003960499432461790)
XLA Ops:
  0.0 0.8 convert_add_fusion.table.refs_4_
  0.9 0.0 copy-start.2
  0.9 1.2 %copy-done.2 = bf16[256,2048]{1,0:T(8,128)(2,1)S(1)} copy-done((bf16[256,2048]{1,0:T(8,128)(2,1)S(1)}, bf16[256,2048]{1,0:T(8,128)(2,1)}, u32[]{:S(2)}) %copy-start.2) | copy-done | bytes 1048600
  2.1 1.5 %decon.1 = (bf16[512,1024]{1,0:T(8,128)(2,1)S(1)}, bf16[512,1024]{1,0:T(8,128)(2,1)S(1)}, f32[32,1,128]{2,1,0:T(1,128)S(1)}) custom-call(bf16[256,2048]{1,0:T(8,128)(2,1)S(1)} %copy-done.2, f32[14,256]{1,0:T(8,128)S(1)} %convert_add_fusion.table.refs_4_), custom_call_target="tpu_custom_call" | custom-call | tf_op jit(solution)/shard_map/decon/pallas_call | solution.py:431
  3.6 0.0 copy-start
  3.6 1.2 %copy-done = bf16[32,8,2048]{2,1,0:T(8,128)(2,1)S(1)} copy-done((bf16[32,8,2048]{2,1,0:T(8,128)(2,1)S(1)}, bf16[32,8,2048]{2,1,0:T(8,128)(2,1)}, u32[]{:S(2)}) %copy-start) | copy-done | bytes 1048600
  4.8 0.0 copy-start.1
  4.8 58.9 %exchange.1 = (f32[32,1,128]{2,1,0:T(1,128)S(1)}, bf16[32,16,1024]{2,1,0:T(8,128)(2,1)S(1)}, f32[8,32,2048]{2,1,0:T(8,128)S(1)}, bf16[2,4,32,1024]{3,2,1,0:T(8,1...) custom-call(bf16[32,16,1024]{2,1,0:T(8,128)(2,1)S(1)} %bitcast.3, ...), custom_call_target="tpu_custom_call" | custom-call | tf_op jit(solution)/shard_map/exchange/pallas_call | solution.py:265
  63.7 2.1 %bin.1 = (bf16[2,4,32,1024]{3,2,1,0:T(8,128)(2,1)S(1)}, bf16[2,4,32,1024]{3,2,1,0:T(8,128)(2,1)S(1)}) custom-call(bf16[32,16,1024]{2,1,0:T(8,128)(2,1)S(1)} %get-tuple-element.26.arrived, f32[32,1,128]{2,1,0:T(1,128)S(1)} %get-tuple-element.27.names), custom_call_target="tpu_custom_call" | custom-call | tf_op jit(solution)/shard_map/bin/pallas_call | solution.py:450
  65.8 4.0 %collective-permute-start = (bf16[2,4,32,1024]{3,2,1,0:T(8,128)(2,1)S(1)}, bf16[2,4,32,1024]{3,2,1,0:T(8,128)(2,1)S(1)}, u32[]{:S(2)}, u32[]{:S(2)}) collective-permute-start(bf16[2,4,32,1024]{3,2,1,0:T(8,128)(2,1)S(1)} %get-tuple-element.28.refs_6_), channel_id=1, source_target_pairs={{0,1},{1,2},{2,3},{3,4},{4,5},{5,6},{6,7},{8,9},{9,10},{10,11},{11... | collective-permute-start | bytes 1572872 | tf_op jit(solution)/shard_map/ppermute | solution.py:459
  69.8 1.9 %collective-permute-start.1 = (bf16[2,4,32,1024]{3,2,1,0:T(8,128)(2,1)S(1)}, bf16[2,4,32,1024]{3,2,1,0:T(8,128)(2,1)S(1)}, u32[]{:S(2)}, u32[]{:S(2)}) collective-permute-start(bf16[2,4,32,1024]{3,2,1,0:T(8,128)(2,1)S(1)} %get-tuple-element.29.refs_5_), channel_id=1, source_target_pairs={{1,0},{2,1},{3,2},{4,3},{5,4},{6,5},{7,6},{9,8},{10,9},{11,10},{12... | collective-permute-start | bytes 1572872 | tf_op jit(solution)/shard_map/ppermute | solution.py:458
  71.7 0.0 copy-done.1
  71.7 10.8 %stack_0.1 = (f32[2,8,896]{2,1,0:T(8,128)S(1)}, bf16[2560,256]{1,0:T(8,128)(2,1)S(1)}) custom-call(bf16[2,4,32,1024]{3,2,1,0:T(8,128)(2,1)S(1)} %get-tuple-element.22.refs_0_, bf16[2,4,32,1024]{3,2,1,0:T(8,128)(2,1)S(1)} %get-tuple-element.23.refs_1_, bf16[2,4,32,1024]{3,2,1,0:T(8,128)(2,1)S(1)} %get-tuple-element.24.refs_2_, ...), custom_call_target="tpu_custom_call" | custom-call | tf_op jit(solution)/shard_map/stack_0/pallas_call | solution.py:482
  82.5 0.0 collective-permute-done.refs_4_
  82.6 0.0 collective-permute-done.1.refs_7_
  82.6 13.8 %stack_1.1 = f32[2,8,2048]{2,1,0:T(8,128)} custom-call(bf16[2,4,32,1024]{3,2,1,0:T(8,128)(2,1)S(1)} %get-tuple-element.22.refs_0_, bf16[2,4,32,1024]{3,2,1,0:T(8,128)(2,1)S(1)} %get-tuple-element.23.refs_1_, bf16[2,4,32,1024]{3,2,1,0:T(8,128)(2,1)S(1)} %get-tuple-element.24.refs_2_, bf16[2,4,32,1024]{3,2,1,0:T(8,128)(2,1)S(1)} %get-tuple-element.25.refs_3_, ...), custom_call_target="tpu_custom_call" | custom-call | tf_op jit(solution)/shard_map/stack_1/pallas_call | solution.py:482
  (2 shorter events, 0.0 us)
Async XLA Ops:
  0.9 1.2 %copy-start.2 = (bf16[256,2048]{1,0:T(8,128)(2,1)S(1)}, bf16[256,2048]{1,0:T(8,128)(2,1)}, u32[]{:S(2)}) copy-start(bf16[256,2048]{1,0:T(8,128)(2,1)} %traces.1) | copy-start | bytes 3145732
  3.6 1.2 %copy-start = (bf16[32,8,2048]{2,1,0:T(8,128)(2,1)S(1)}, bf16[32,8,2048]{2,1,0:T(8,128)(2,1)}, u32[]{:S(2)}) copy-start(bf16[32,8,2048]{2,1,0:T(8,128)(2,1)} %nmo_weights.1) | copy-start | bytes 3145732
  4.8 66.9 %copy-start.1 = (s32[32,2048]{1,0:T(8,128)S(1)}, s32[32,2048]{1,0:T(8,128)}, u32[]{:S(2)}) copy-start(s32[32,2048]{1,0:T(8,128)} %refs_10_.1) | copy-start | bytes 786436
  65.8 16.8 %collective-permute-start = (bf16[2,4,32,1024]{3,2,1,0:T(8,128)(2,1)S(1)}, bf16[2,4,32,1024]{3,2,1,0:T(8,128)(2,1)S(1)}, u32[]{:S(2)}, u32[]{:S(2)}) collective-permute-start(bf16[2,4,32,1024]{3,2,1,0:T(8,128)(2,1)S(1)} %get-tuple-element.28.refs_6_), channel_id=1, source_target_pairs={{0,1},{1,2},{2,3},{3,4},{4,5},{5,6},{6,7},{8,9},{9,10},{10,11},{11... | collective-permute-start | bytes 1572872 | tf_op jit(solution)/shard_map/ppermute | solution.py:459
  69.8 12.8 %collective-permute-start.1 = (bf16[2,4,32,1024]{3,2,1,0:T(8,128)(2,1)S(1)}, bf16[2,4,32,1024]{3,2,1,0:T(8,128)(2,1)S(1)}, u32[]{:S(2)}, u32[]{:S(2)}) collective-permute-start(bf16[2,4,32,1024]{3,2,1,0:T(8,128)(2,1)S(1)} %get-tuple-element.29.refs_5_), channel_id=1, source_target_pairs={{1,0},{2,1},{3,2},{4,3},{5,4},{6,5},{7,6},{9,8},{10,9},{11,10},{12... | collective-permute-start | bytes 1572872 | tf_op jit(solution)/shard_map/ppermute | solution.py:458

commit v6 on v5

--- a/solution.py
+++ b/solution.py
@@ -72,13 +72,14 @@
                     traces[rows, window], matrix, preferred_element_type=jnp.float32
                 )
             dec[rows, lanes] = (product * factor).astype(jnp.bfloat16)
-    span = samples // len(outs)
-    for part, out in enumerate(outs):
-        for lane in range(0, span, 256):
-            place = part * span + lane
+    first = 0
+    for out in outs:
+        for lane in range(0, out.shape[1], 256):
+            place = first + lane
             out[:, lane : lane + 256] = jnp.dot(
                 pick, dec[:, place : place + 256], preferred_element_type=jnp.float32
             ).astype(jnp.bfloat16)
+        first += out.shape[1]
 
 
 def exchange_kernel(
@@ -90,14 +91,18 @@
     names,
     rows_1,
     nmo_weights,
+    weights,
+    lo_0,
+    hi_0,
+    left_0,
+    right_0,
+    lo_1,
+    hi_1,
+    left_1,
+    right_1,
     names_in,
+    arrived_0,
     arrived_1,
-    weights,
-    lo,
-    hi,
-    left,
-    right,
-    arrived_0,
     send_sems,
     recv_sems,
     own_sem,
@@ -180,37 +185,45 @@
 
     @pl.when(bin_here == 0)
     def _():
-        left[...] = jnp.zeros(left.shape, left.dtype)
+        for left in (left_0, left_1):
+            left[...] = jnp.zeros(left.shape, left.dtype)
 
     @pl.when(bin_here == bins - 1)
     def _():
-        right[...] = jnp.zeros(right.shape, right.dtype)
+        for right in (right_0, right_1):
+            right[...] = jnp.zeros(right.shape, right.dtype)
+
+    def send_rims(lo, hi, left, right, sem):
+        @pl.when(bin_here < bins - 1)
+        def _():
+            rim_copy(hi, left, sem, 1).start()
+
+        @pl.when(bin_here > 0)
+        def _():
+            rim_copy(lo, right, sem + 2, -1).start()
+
+    def await_rims(lo, hi, left, right, sem):
+        @pl.when(bin_here < bins - 1)
+        def _():
+            rim_copy(hi, left, sem, 1).wait_send()
+            rim_copy(lo, right, sem + 2, 1).wait_recv()
+
+        @pl.when(bin_here > 0)
+        def _():
+            rim_copy(lo, right, sem + 2, -1).wait_send()
+            rim_copy(hi, left, sem, -1).wait_recv()
 
     own[0].wait()
     own[1].wait()
     each((0, 1), lambda copy: copy.wait())
-    bin_rows(capacity, cells_here, arrived_0, names_in, lo, hi)
-
-    @pl.when(bin_here < bins - 1)
-    def _():
-        rim_copy(hi, left, 0, 1).start()
-
-    @pl.when(bin_here > 0)
-    def _():
-        rim_copy(lo, right, 2, -1).start()
-
+    bin_rows(capacity, cells_here, arrived_0, names_in, lo_0, hi_0)
+    send_rims(lo_0, hi_0, left_0, right_0, 0)
     own[2].wait()
     each((2,), lambda copy: copy.wait())
-
-    @pl.when(bin_here < bins - 1)
-    def _():
-        rim_copy(hi, left, 0, 1).wait_send()
-        rim_copy(lo, right, 2, 1).wait_recv()
-
-    @pl.when(bin_here > 0)
-    def _():
-        rim_copy(lo, right, 2, -1).wait_send()
-        rim_copy(hi, left, 0, -1).wait_recv()
+    bin_rows(capacity, cells_here, arrived_1, names_in, lo_1, hi_1)
+    send_rims(lo_1, hi_1, left_1, right_1, 4)
+    await_rims(lo_0, hi_0, left_0, right_0, 0)
+    await_rims(lo_1, hi_1, left_1, right_1, 4)
 
 
 def bin_rows(capacity, cells_here, arrived, names, lo, hi):
@@ -253,31 +266,26 @@
         matrix[256 * tap + 256 : 256 * tap + 512, 128:] = one
 
 
-def exchange(rows_0, names, rows_1, nmo_weights, cells_here, rim):
+def exchange(rows_0, names, rows_1, nmo_weights, cells_here, rims):
     shots, bins = lax.axis_size("shot"), lax.axis_size("bin")
     count = shots * bins
     offsets, taps, samples = nmo_weights.shape
 
-    def like(array):
-        return jax.ShapeDtypeStruct(array.shape, array.dtype)
-
     vmem = pl.BlockSpec(memory_space=pltpu.VMEM)
     return pl.pallas_call(
         functools.partial(exchange_kernel, shots, bins, rows_0.shape[1], cells_here),
-        out_shape=[
-            like(names),
-            like(rows_1),
-            jax.ShapeDtypeStruct((taps, offsets, samples), jnp.float32),
-        ]
-        + [rim] * 4,
+        out_shape=[jax.ShapeDtypeStruct((taps, offsets, samples), jnp.float32)]
+        + [rim for rim in rims for _ in range(4)],
         in_specs=[vmem] * 4,
-        out_specs=[vmem] * 7,
+        out_specs=[vmem] * 9,
         scratch_shapes=[
+            pltpu.VMEM(names.shape, names.dtype),
             pltpu.VMEM(rows_0.shape, rows_0.dtype),
+            pltpu.VMEM(rows_1.shape, rows_1.dtype),
             pltpu.SemaphoreType.DMA((3, count)),
             pltpu.SemaphoreType.DMA((3, count)),
             pltpu.SemaphoreType.DMA((3,)),
-            pltpu.SemaphoreType.DMA((4,)),
+            pltpu.SemaphoreType.DMA((8,)),
         ],
         compiler_params=pltpu.CompilerParams(
             collective_id=1, has_side_effects=True, vmem_limit_bytes=VMEM_BYTES
@@ -286,13 +294,10 @@
     )(rows_0, names, rows_1, nmo_weights)
 
 
-def stack_kernel(taps, first_block, dip_row, halves, *refs):
+def stack_kernel(taps, dip_row, halves, *refs):
     inputs = refs[: 4 * len(halves)]
     rest = refs[4 * len(halves) :]
-    if first_block:
-        earlier, matrix, start, weights, out, ext, ring, staged, sems = rest
-    else:
-        table, start, weights, out, matrix, ext, ring, staged, sems = rest
+    table, start, weights, out, matrix, ext, ring, staged, sems = rest
     crosslines, offsets = ext.shape[1], ext.shape[2]
     blocks = ext.shape[3] // 128 - 2
     half = crosslines // 4
@@ -314,10 +319,7 @@
             ext[:, :, :, low:high] = jnp.zeros(
                 (IL_DEV, crosslines, offsets, high - low), jnp.bfloat16
             )
-    if not first_block:
-        dip_matrix(table[dip_row : dip_row + taps, :256], matrix)
-    else:
-        out[:, :, : 128 * first_block] = earlier[...]
+    dip_matrix(table[dip_row : dip_row + taps, :256], matrix)
     for copy in copies:
         copy.wait()
 
@@ -345,11 +347,11 @@
     def stack_block(block, carry):
         filter_block(jnp.minimum(block + 2, blocks), staged)
         this, following = lax.rem(block, 3), lax.rem(block + 1, 3)
-        lanes = pl.ds(pl.multiple_of(128 * (block + first_block), 128), 128)
+        lanes = pl.ds(pl.multiple_of(128 * block, 128), 128)
         totals = [jnp.zeros((8, 128), jnp.float32) for _ in range(IL_DEV * XL_DEV)]
         for first in range(0, offsets, 8):
             group = slice(first, first + 8)
-            at = start[group, lanes] - (128 * (block + first_block) - 64)
+            at = start[group, lanes] - (128 * block - 64)
             for tap in range(nmo_taps):
                 moved = at + tap
                 index = moved & 127
@@ -399,9 +401,8 @@
     anywhere = pl.BlockSpec(memory_space=pl.ANY)
     params = pltpu.CompilerParams(vmem_limit_bytes=VMEM_BYTES)
 
-    parts = 2
-    span = samples // parts
-    row = jax.ShapeDtypeStruct((slots, span), jnp.bfloat16)
+    spans = (samples - samples // 1024 * 256, samples // 1024 * 256)
+    rows = [jax.ShapeDtypeStruct((slots, span), jnp.bfloat16) for span in spans]
     width = max(trace_count, 256)
 
     taps, time_taps = dip_filter.shape
@@ -430,9 +431,9 @@
     )
     *outgoing, codes = pl.pallas_call(
         functools.partial(decon_kernel, owners, capacity, offsets, shot_filter.shape[0]),
-        out_shape=[row] * parts + [jax.ShapeDtypeStruct((owners, 1, 128), jnp.float32)],
+        out_shape=rows + [jax.ShapeDtypeStruct((owners, 1, 128), jnp.float32)],
         in_specs=[vmem] * 2,
-        out_specs=[vmem] * (parts + 1),
+        out_specs=[vmem] * (len(spans) + 1),
         scratch_shapes=[
             pltpu.VMEM(traces.shape, jnp.bfloat16),
         ],
@@ -441,62 +442,32 @@
     )(traces, table)
 
     crosslines = 2 * XL_DEV
-    rim = jax.ShapeDtypeStruct((IL_DEV, half, offsets, span), jnp.bfloat16)
-    rows_0, rows_1 = (rows.reshape(owners, capacity, span) for rows in outgoing)
-    codes, arrived, weights, lo, hi, left, right = exchange(
-        rows_0, codes, rows_1, nmo_weights, cells_here, rim
-    )
-    sides = [(left, lo, hi, right)]
-    lo, hi = pl.pallas_call(
-        functools.partial(bin_rows, capacity, cells_here),
-        out_shape=(rim, rim),
-        in_specs=[vmem] * 2,
-        out_specs=(vmem, vmem),
+    rims = [
+        jax.ShapeDtypeStruct((IL_DEV, half, offsets, span), jnp.bfloat16) for span in spans
+    ]
+    rows_0, rows_1 = (
+        rows.reshape(owners, capacity, span) for rows, span in zip(outgoing, spans)
+    )
+    weights, lo_0, hi_0, left_0, right_0, lo_1, hi_1, left_1, right_1 = exchange(
+        rows_0, codes, rows_1, nmo_weights, cells_here, rims
+    )
+    operands = (left_0, lo_0, hi_0, right_0, left_1, lo_1, hi_1, right_1)
+    pieces = ((0, 128, spans[0]), (0, 128 + spans[0], spans[1]))
+    return pl.pallas_call(
+        functools.partial(stack_kernel, taps, dip_row, pieces),
+        out_shape=jax.ShapeDtypeStruct((IL_DEV, XL_DEV, samples), jnp.float32),
+        in_specs=[anywhere] * len(operands) + [vmem] * 3,
+        out_specs=vmem,
+        scratch_shapes=[
+            pltpu.VMEM(((taps + 1) * 256, 256), jnp.bfloat16),
+            pltpu.VMEM((IL_DEV, crosslines, offsets, samples + 256), jnp.bfloat16),
+            pltpu.VMEM((3, IL_DEV, XL_DEV // 2, 2, offsets, 128), jnp.float32),
+            pltpu.VMEM((IL_DEV, XL_DEV // 2, 2, offsets, 128), jnp.float32),
+            pltpu.SemaphoreType.DMA((len(operands),)),
+        ],
         compiler_params=params,
-        name="bin",
-    )(arrived, codes)
-    right = lax.ppermute(lo, "bin", [(i + 1, i) for i in range(bins - 1)])
-    left = lax.ppermute(hi, "bin", [(i, i + 1) for i in range(bins - 1)])
-    sides.append((left, lo, hi, right))
-
-    per_part = span // 128
-    total = samples // 128
-    stacked = None
-    for part in range(parts):
-        first = max(per_part * part - 1, 0)
-        last = per_part * (part + 1) - 1 if part < parts - 1 else total
-        blocks = last - first
-        low = first - 1
-        operands, halves = [], []
-        for piece in range(parts):
-            begin = max(low, per_part * piece)
-            end = min(last + 1, per_part * (piece + 1))
-            if begin < end and piece <= part:
-                operands += sides[piece]
-                halves.append(
-                    (128 * (begin - per_part * piece), 128 * (begin - low), 128 * (end - begin))
-                )
-        result = jax.ShapeDtypeStruct((IL_DEV, XL_DEV, 128 * last), jnp.float32)
-        bands = jax.ShapeDtypeStruct(((taps + 1) * 256, 256), jnp.bfloat16)
-        extra = (stacked, matrix) if first else (table,)
-        made = pl.pallas_call(
-            functools.partial(stack_kernel, taps, first, dip_row, halves),
-            out_shape=[result] if first else [result, bands],
-            in_specs=[anywhere] * len(operands) + [vmem] * (len(extra) + 2),
-            out_specs=[vmem] * (1 if first else 2),
-            scratch_shapes=[
-                pltpu.VMEM((IL_DEV, crosslines, offsets, 128 * (blocks + 2)), jnp.bfloat16),
-                pltpu.VMEM((3, IL_DEV, XL_DEV // 2, 2, offsets, 128), jnp.float32),
-                pltpu.VMEM((IL_DEV, XL_DEV // 2, 2, offsets, 128), jnp.float32),
-                pltpu.SemaphoreType.DMA((4 * len(halves),)),
-            ],
-            compiler_params=params,
-            name=f"stack_{part}",
-        )(*operands, *extra, nmo_start, weights)
-        stacked = made[0]
-        if not first:
-            matrix = made[1]
-    return stacked
+        name="stack",
+    )(*operands, table, nmo_start, weights)
 
 
 def solution(mesh):

time: 97.5 us -> 104 us (1.067)
  Pallas kernels: 87.1 us -> 99.4 us
  starting transfers between devices: 5.92 us -> 0 us
    pallas_call x1, Pallas kernels: 58.9 us -> 74.5 us  [exchange(): pl.pallas_call(functools.partial(exchange_kernel, shots, bins, rows_0.sha...]
    ppermute x2 -> x0, starting transfers between devices: 5.92 us -> none  [the longest x1 4 us: per_device(): left = lax.ppermute(hi, 'bin', [(i, i + 1) for i in range(bins - 1)])]
    pallas_call x3 -> x1, Pallas kernels: 26.8 us -> 23.4 us  [per_device(): pl.pallas_call(functools.partial(stack_kernel, taps, dip_row, pieces), ou...]
  transfers between devices with their start and end apart: 2 -> 0, of which waited for: 0 -> 0; matrix products, arithmetic and copies ran while one was open for 0% -> 0% of each run, Pallas kernels for 11% -> 0%
where the time goes in v6:
time: 104 us; the launch traced here: 103 us
  Pallas kernels  99.4 us (96%)
  local copies, waits for them, and re-layouts  2.44 us (2%)
    pallas_call x1, Pallas kernels, exchange(): pl.pallas_call(functools.partial(exchange_kernel, shots, bins, rows_0.sha...  74.5 us
    pallas_call x1, Pallas kernels, per_device(): pl.pallas_call(functools.partial(stack_kernel, taps, dip_row, pieces), ou...  23.4 us
    unnamed x6, local copies, waits for them, and re-layouts  2.44 us

profile of v6, /device:TPU:11, one launch (start us, length us, event | category | flops | bytes accessed | tf_op | source)
XLA Modules:
  0.0 102.7 jit_solution(12233929776189238632)
XLA Ops:
  0.0 0.8 convert_add_fusion.table.refs_8_
  0.9 0.0 copy-start.1
  0.9 1.2 %copy-done.1 = bf16[256,2048]{1,0:T(8,128)(2,1)S(1)} copy-done((bf16[256,2048]{1,0:T(8,128)(2,1)S(1)}, bf16[256,2048]{1,0:T(8,128)(2,1)}, u32[]{:S(2)}) %copy-start.1) | copy-done | bytes 1048600
  2.1 0.0 copy-start.2
  2.1 1.5 %decon.1 = (bf16[512,1536]{1,0:T(8,128)(2,1)S(1)}, bf16[512,512]{1,0:T(8,128)(2,1)S(1)}, f32[32,1,128]{2,1,0:T(1,128)S(1)}) custom-call(bf16[256,2048]{1,0:T(8,128)(2,1)S(1)} %copy-done.1, f32[14,256]{1,0:T(8,128)S(1)} %convert_add_fusion.table.refs_8_), custom_call_target="tpu_custom_call" | custom-call | tf_op jit(solution)/shard_map/decon/pallas_call | solution.py:432
  3.6 0.0 copy-start
  3.6 1.2 %copy-done = bf16[32,8,2048]{2,1,0:T(8,128)(2,1)S(1)} copy-done((bf16[32,8,2048]{2,1,0:T(8,128)(2,1)S(1)}, bf16[32,8,2048]{2,1,0:T(8,128)(2,1)}, u32[]{:S(2)}) %copy-start) | copy-done | bytes 1048600
  4.8 74.5 %exchange.1 = (f32[8,32,2048]{2,1,0:T(8,128)S(1)}, bf16[2,4,32,1536]{3,2,1,0:T(8,128)(2,1)S(1)}, bf16[2,4,32,1536]{3,2,1,0:T(8,128)(2,1)S(1)}, bf16[2,4,32,1536]...) custom-call(bf16[32,16,1536]{2,1,0:T(8,128)(2,1)S(1)} %bitcast.3, ...), custom_call_target="tpu_custom_call" | custom-call | tf_op jit(solution)/shard_map/exchange/pallas_call | solution.py:275
  79.3 0.0 copy-done.2
  79.3 23.4 %stack.1 = f32[2,8,2048]{2,1,0:T(8,128)} custom-call(bf16[2,4,32,1536]{3,2,1,0:T(8,128)(2,1)S(1)} %get-tuple-element.20.refs_0_, bf16[2,4,32,1536]{3,2,1,0:T(8,128)(2,1)S(1)} %get-tuple-element.21.refs_1_, bf16[2,4,32,1536]{3,2,1,0:T(8,128)(2,1)S(1)} %get-tuple-element.22.refs_2_, bf16[2,4,32,1536]{3,2,1,0:T(8,128)(2,1)S(1)} %get-tuple-element.23.refs_3_, ...), custom_call_target="tpu_custom_call" | custom-call | tf_op jit(solution)/shard_map/stack/pallas_call | solution.py:456
  (2 shorter events, 0.0 us)
Async XLA Ops:
  0.9 1.2 %copy-start.1 = (bf16[256,2048]{1,0:T(8,128)(2,1)S(1)}, bf16[256,2048]{1,0:T(8,128)(2,1)}, u32[]{:S(2)}) copy-start(bf16[256,2048]{1,0:T(8,128)(2,1)} %traces.1) | copy-start | bytes 3145732
  2.1 77.2 %copy-start.2 = (s32[32,2048]{1,0:T(8,128)S(1)}, s32[32,2048]{1,0:T(8,128)}, u32[]{:S(2)}) copy-start(s32[32,2048]{1,0:T(8,128)} %refs_9_.1) | copy-start | bytes 786436
  3.6 1.2 %copy-start = (bf16[32,8,2048]{2,1,0:T(8,128)(2,1)S(1)}, bf16[32,8,2048]{2,1,0:T(8,128)(2,1)}, u32[]{:S(2)}) copy-start(bf16[32,8,2048]{2,1,0:T(8,128)(2,1)} %nmo_weights.1) | copy-start | bytes 3145732
